TPU v7x, 256 devices: a whole 4x4x8 slice. The times are simulated.
256 devices in a mesh: outer: 64 (over x_hi, z, y), inner: 4 (over x_lo, core).
Axes of the slice: x: 4 (x_hi: 2, x_lo: 2; x = x_hi * 2 + x_lo), y: 4, z: 8, core: 2. Of those that a mesh axis runs over, the one named last changes fastest.
Arguments:
- tokens: bfloat16 [32768, 2560], P(('outer', 'inner')), may hold values from -6 to 6
- norm_gain: float32 [2560], replicated, may hold values from 0.1 to 1.9
- w_query: bfloat16 [2560, 2560], P(None, 'inner'), may hold values from -0.15625 to 0.15625
- b_query: float32 [2560], P('inner'), may hold values from -24 to 24
- w_key: bfloat16 [2560, 512], P(None, 'inner'), may hold values from -0.25 to 0.25
- b_key: float32 [512], P('inner'), may hold values from -40 to 40
- w_value: bfloat16 [2560, 512], P(None, 'inner'), may hold values from -0.125 to 0.125
- b_value: float32 [512], P('inner'), may hold values from -3 to 3
- w_out: bfloat16 [2560, 2560], P('inner'), may hold values from -0.125 to 0.125
- positions: int32 [32768], P(('outer', 'inner')), may hold values from 0 to 32767, as said below
Outputs:
- attended: bfloat16 [32768, 2560], P(('outer', 'inner'))
Inputs may be any that keep to these rules, and one draw needn't show every extreme that they name: Block b holds two whole runs of 256 consecutive positions in order: run c in its first half and run 2 * 64 - 1 - c in its second, where c differs from block to block; every position occurs once.
All inputs are finite; a program needn't handle non-finite values.
Results may differ from a plain program's by a relative error of at most 0.017.
The roundings to bfloat16 on the way count: a program that leaves them out, or rounds other values in their place, can miss the bound.
Values may be sent and summed in bfloat16 or wider, within the bound.
No kernel may reach another device: no remote copies, remote signals or barrier semaphores. Data moves between devices by JAX's collectives and lax.ppermute only.
A program may use at most 64 MiB of HBM per device.

v0:
```python
import jax
import jax.numpy as jnp
from jax import lax
from jax.sharding import PartitionSpec as P

HEAD_DIM = 128
VISITS = 14


rope_base = 10000000.0
norm_eps = 1e-06
masked_score = -1e30


def shifted(block, axis, distance):
    devices = range(lax.axis_size(axis))
    route = [((i - distance) % len(devices), i) for i in devices]
    return lax.ppermute(block, axis, route)


def normalize(tokens, norm_gain):
    values = tokens.astype(jnp.float32)
    scale = lax.rsqrt(jnp.mean(values * values, axis=-1, keepdims=True) + norm_eps)
    return (values * scale * norm_gain).astype(jnp.bfloat16)


def angles_for(places, head_dim):
    inverse = rope_base ** (-(jnp.arange(head_dim // 2, dtype=jnp.float32) * 2.0 / head_dim))
    return places.astype(jnp.float32)[:, None] * inverse[None, :]


def rotate(heads, angles):
    half_dim = heads.shape[-1] // 2
    cosine = jnp.cos(angles)[:, None, :]
    sine_term = jnp.sin(angles)[:, None, :]
    leading = heads[..., :half_dim]
    trailing = heads[..., half_dim:]
    return jnp.concatenate(
        [leading * cosine - trailing * sine_term, trailing * cosine + leading * sine_term], -1
    )


def places_from(run_value, block_rows, outer_size):
    half_rows = block_rows // 2
    run_first = run_value.astype(jnp.int32)
    row_index = jnp.arange(block_rows, dtype=jnp.int32)
    run_here = jnp.where(row_index >= half_rows, 2 * outer_size - 1 - run_first, run_first)
    return run_here * half_rows + row_index % half_rows


def local(tokens, norm_gain, w_query, b_query, w_key, b_key, w_value, b_value, w_out, positions):
    head_dim = HEAD_DIM
    rows_dev = tokens.shape[0]
    inner_size = lax.axis_size("inner")
    outer_size = lax.axis_size("outer")
    block_rows = rows_dev * inner_size
    query_cols = w_query.shape[1]
    key_cols = w_key.shape[1]
    local_queries = query_cols // head_dim
    local_keys = key_cols // head_dim
    group_size = local_queries // local_keys
    visit_count = min(VISITS, outer_size)
    score_scale = head_dim ** (-0.5)
    block_places = lax.all_gather(positions, "inner", axis=0, tiled=True)
    own_run = (block_places[0:1] // (block_rows // 2)).astype(jnp.float32).astype(jnp.bfloat16)
    angles = angles_for(block_places, head_dim)
    normed = normalize(tokens, norm_gain)
    piece = lax.all_gather(normed, "inner", axis=0, tiled=True)
    projected = jnp.concatenate(
        [
            jnp.dot(piece, w_query, preferred_element_type=jnp.float32),
            jnp.dot(piece, w_key, preferred_element_type=jnp.float32),
            jnp.dot(piece, w_value, preferred_element_type=jnp.float32),
        ],
        1,
    )
    key_heads = rotate(
        (projected[:, query_cols : query_cols + key_cols] + b_key).reshape(
            block_rows, local_keys, head_dim
        ),
        angles,
    ).astype(jnp.bfloat16)
    value_heads = (
        (projected[:, query_cols + key_cols :] + b_value)
        .reshape(block_rows, local_keys, head_dim)
        .astype(jnp.bfloat16)
    )
    key_heads, value_heads = (key_heads, value_heads)
    rotated = rotate(
        (projected[:, :query_cols] + b_query).reshape(block_rows, local_queries, head_dim), angles
    )
    queries = rotated.astype(jnp.bfloat16).reshape(block_rows, local_keys, group_size, head_dim)

    def attend(running, key_blk, value_blk, key_places):
        peak_score, denominator, weighted = running
        scores = (
            jnp.einsum("qhgd,khd->hgqk", queries, key_blk, preferred_element_type=jnp.float32)
            * score_scale
        )
        visible = key_places[None, :] <= block_places[:, None]
        scores = jnp.where(visible[None, None], scores, masked_score)
        new_peak = jnp.maximum(peak_score, jnp.max(scores, axis=-1))
        factor = jnp.exp(peak_score - new_peak)
        exponent = jnp.exp(scores - new_peak[..., None])
        denominator = denominator * factor + jnp.sum(exponent, axis=-1)
        weights = exponent.astype(jnp.bfloat16)
        weighted = weighted * factor[..., None] + jnp.einsum(
            "hgqk,khd->hgqd", weights, value_blk, preferred_element_type=jnp.float32
        )
        return (new_peak, denominator, weighted)

    initial = (
        jnp.full((local_keys, group_size, block_rows), masked_score, jnp.float32),
        jnp.zeros((local_keys, group_size, block_rows), jnp.float32),
        jnp.zeros((local_keys, group_size, block_rows, head_dim), jnp.float32),
    )
    running = attend(initial, key_heads, value_heads, block_places)

    def advance(turn_index, carried):
        key_blk, value_blk, run_blk, state_now = carried
        key_blk, value_blk, run_blk = shifted((key_blk, value_blk, run_blk), "outer", 1)
        key_places = places_from(run_blk[0], block_rows, outer_size)
        return (key_blk, value_blk, run_blk, attend(state_now, key_blk, value_blk, key_places))

    carried = lax.fori_loop(1, visit_count, advance, (key_heads, value_heads, own_run, running))
    running = carried[3]
    peak_score, denominator, weighted = running
    mixed_heads = (weighted / denominator[..., None]).transpose(2, 0, 1, 3)
    mixed_heads = mixed_heads.reshape(block_rows, query_cols).astype(jnp.bfloat16)
    return lax.psum_scatter(
        jnp.dot(mixed_heads, w_out, preferred_element_type=jnp.float32).astype(jnp.bfloat16),
        "inner",
        scatter_dimension=0,
        tiled=True,
    )


def solution(mesh):
    in_specs = (
        P(("outer", "inner"), None),
        P(),
        P(None, "inner"),
        P("inner"),
        P(None, "inner"),
        P("inner"),
        P(None, "inner"),
        P("inner"),
        P("inner", None),
        P(("outer", "inner")),
    )
    out_specs = P(("outer", "inner"), None)
    return jax.shard_map(local, mesh=mesh, in_specs=in_specs, out_specs=out_specs, check_vma=False)
```

profile of v0, /device:TPU:1, one launch (start us, length us, event | category | flops | bytes accessed | tf_op | source)
XLA Modules:
  0.0 417.9 jit_solution(1749015162092237672)
XLA Ops:
  10.2 8.1 %all-gather = s32[4,1,128]{2,1,0:T(1,128)S(1)} all-gather(s32[1,1,128]{2,1,0:T(1,128)S(1)} %bitcast.151), channel_id=1, replica_groups=mesh['outer'=64,'inner'=4] {'inner'}, dimensions={0}, use_global_device_ids=true | all-gather | bytes 2560 | tf_op jit(solution)/shard_map/all_gather | solution.py:64
  23.5 27.1 %all-gather.3.cloned.1.call-done = bf16[512,2560]{1,0:T(8,128)(2,1)} async-done(((bf16[128,2560]{1,0:T(8,128)(2,1)}), bf16[512,2560]{1,0:T(8,128)(2,1)}) %all-gather.3.cloned.1.call-update) | async-done | bytes 2621456 | tf_op jit(solution)/shard_map/all_gather | solution.py:68
  57.0 6.0 %convolution_add_fusion = f32[512,640]{1,0:T(8,128)} fusion(bf16[512,2560]{1,0:T(8,128)(2,1)} %all-gather.3.cloned.1.call-done, bf16[2560,640]{1,0:T(8,128)(2,1)} %param.14, f32[640]{0:T(1024)} %param.15), kind=kOutput, calls=%fused_computation.41 | convolution fusion | flops 1678049280 | bytes 7211520 | tf_op jit(solution)/shard_map/dot_general | solution.py:71
  83.7 275.4 %while.22 = (s32[]{:T(128)}, bf16[512,1,128]{2,0,1:T(8,128)(2,1)}, bf16[512,1,128]{2,0,1:T(8,128)(2,1)}, bf16[1]{0:T(256)(128)(2,1)}, f32[1,5,512]{2,1,0:T(8,128...) while((s32[]{:T(128)}, bf16[512,1,128]{2,0,1:T(8,128)(2,1)}, ...), condition=%wide.region_6.7_spmd, body=%wide.region_3.6_spmd.sunk | while | flops 686436864 | bytes 32627068 | solution.py:125
  86.1 4.9 %collective-permute-start.2 = (bf16[1]{0:T(256)(128)(2,1)}, bf16[1]{0:T(256)(128)(2,1)}, u32[]{:S(2)}, u32[]{:S(2)}) collective-permute-start(bf16[1]{0:T(256)(128)(2,1)} %copy.49), channel_id=1, source_target_pairs={{252,0},{0,4},{4,8},{8,12},{12,16},{16,20},{20,24},{24,28},{28,32}... | collective-permute-start | bytes 14 | tf_op jit(solution)/shard_map/while/body/eval_jaxpr/ppermute | solution.py:18
  91.0 6.8 %collective-permute-done.2 = bf16[1]{0:T(256)(128)(2,1)} collective-permute-done((bf16[1]{0:T(256)(128)(2,1)}, bf16[1]{0:T(256)(128)(2,1)}, u32[]{:S(2)}, u32[]{:S(2)}) %collective-permute-start.2) | collective-permute-done | bytes 34 | tf_op jit(solution)/shard_map/while/body/eval_jaxpr/ppermute | solution.py:18
  107.5 5.3 %collective-permute-start.2 = (bf16[1]{0:T(256)(128)(2,1)}, bf16[1]{0:T(256)(128)(2,1)}, u32[]{:S(2)}, u32[]{:S(2)}) collective-permute-start(bf16[1]{0:T(256)(128)(2,1)} %copy.49), channel_id=1, source_target_pairs={{252,0},{0,4},{4,8},{8,12},{12,16},{16,20},{20,24},{24,28},{28,32}... | collective-permute-start | bytes 14 | tf_op jit(solution)/shard_map/while/body/eval_jaxpr/ppermute | solution.py:18
  112.8 7.5 %collective-permute-done.2 = bf16[1]{0:T(256)(128)(2,1)} collective-permute-done((bf16[1]{0:T(256)(128)(2,1)}, bf16[1]{0:T(256)(128)(2,1)}, u32[]{:S(2)}, u32[]{:S(2)}) %collective-permute-start.2) | collective-permute-done | bytes 34 | tf_op jit(solution)/shard_map/while/body/eval_jaxpr/ppermute | solution.py:18
  130.0 4.1 collective-permute-start.2
  134.1 7.5 %collective-permute-done.2 = bf16[1]{0:T(256)(128)(2,1)} collective-permute-done((bf16[1]{0:T(256)(128)(2,1)}, bf16[1]{0:T(256)(128)(2,1)}, u32[]{:S(2)}, u32[]{:S(2)}) %collective-permute-start.2) | collective-permute-done | bytes 34 | tf_op jit(solution)/shard_map/while/body/eval_jaxpr/ppermute | solution.py:18
  151.4 3.5 collective-permute-start.2
  154.9 7.5 %collective-permute-done.2 = bf16[1]{0:T(256)(128)(2,1)} collective-permute-done((bf16[1]{0:T(256)(128)(2,1)}, bf16[1]{0:T(256)(128)(2,1)}, u32[]{:S(2)}, u32[]{:S(2)}) %collective-permute-start.2) | collective-permute-done | bytes 34 | tf_op jit(solution)/shard_map/while/body/eval_jaxpr/ppermute | solution.py:18
  172.2 3.5 collective-permute-start.2
  175.7 7.5 %collective-permute-done.2 = bf16[1]{0:T(256)(128)(2,1)} collective-permute-done((bf16[1]{0:T(256)(128)(2,1)}, bf16[1]{0:T(256)(128)(2,1)}, u32[]{:S(2)}, u32[]{:S(2)}) %collective-permute-start.2) | collective-permute-done | bytes 34 | tf_op jit(solution)/shard_map/while/body/eval_jaxpr/ppermute | solution.py:18
  193.0 3.5 collective-permute-start.2
  196.5 7.5 %collective-permute-done.2 = bf16[1]{0:T(256)(128)(2,1)} collective-permute-done((bf16[1]{0:T(256)(128)(2,1)}, bf16[1]{0:T(256)(128)(2,1)}, u32[]{:S(2)}, u32[]{:S(2)}) %collective-permute-start.2) | collective-permute-done | bytes 34 | tf_op jit(solution)/shard_map/while/body/eval_jaxpr/ppermute | solution.py:18
  213.7 3.5 collective-permute-start.2
  217.3 7.5 %collective-permute-done.2 = bf16[1]{0:T(256)(128)(2,1)} collective-permute-done((bf16[1]{0:T(256)(128)(2,1)}, bf16[1]{0:T(256)(128)(2,1)}, u32[]{:S(2)}, u32[]{:S(2)}) %collective-permute-start.2) | collective-permute-done | bytes 34 | tf_op jit(solution)/shard_map/while/body/eval_jaxpr/ppermute | solution.py:18
  234.5 3.5 collective-permute-start.2
  238.1 7.5 %collective-permute-done.2 = bf16[1]{0:T(256)(128)(2,1)} collective-permute-done((bf16[1]{0:T(256)(128)(2,1)}, bf16[1]{0:T(256)(128)(2,1)}, u32[]{:S(2)}, u32[]{:S(2)}) %collective-permute-start.2) | collective-permute-done | bytes 34 | tf_op jit(solution)/shard_map/while/body/eval_jaxpr/ppermute | solution.py:18
  255.3 3.5 collective-permute-start.2
  258.8 7.5 %collective-permute-done.2 = bf16[1]{0:T(256)(128)(2,1)} collective-permute-done((bf16[1]{0:T(256)(128)(2,1)}, bf16[1]{0:T(256)(128)(2,1)}, u32[]{:S(2)}, u32[]{:S(2)}) %collective-permute-start.2) | collective-permute-done | bytes 34 | tf_op jit(solution)/shard_map/while/body/eval_jaxpr/ppermute | solution.py:18
  276.1 3.5 collective-permute-start.2
  279.6 7.5 %collective-permute-done.2 = bf16[1]{0:T(256)(128)(2,1)} collective-permute-done((bf16[1]{0:T(256)(128)(2,1)}, bf16[1]{0:T(256)(128)(2,1)}, u32[]{:S(2)}, u32[]{:S(2)}) %collective-permute-start.2) | collective-permute-done | bytes 34 | tf_op jit(solution)/shard_map/while/body/eval_jaxpr/ppermute | solution.py:18
  296.9 3.5 collective-permute-start.2
  300.4 7.5 %collective-permute-done.2 = bf16[1]{0:T(256)(128)(2,1)} collective-permute-done((bf16[1]{0:T(256)(128)(2,1)}, bf16[1]{0:T(256)(128)(2,1)}, u32[]{:S(2)}, u32[]{:S(2)}) %collective-permute-start.2) | collective-permute-done | bytes 34 | tf_op jit(solution)/shard_map/while/body/eval_jaxpr/ppermute | solution.py:18
  317.7 3.5 collective-permute-start.2
  321.2 7.5 %collective-permute-done.2 = bf16[1]{0:T(256)(128)(2,1)} collective-permute-done((bf16[1]{0:T(256)(128)(2,1)}, bf16[1]{0:T(256)(128)(2,1)}, u32[]{:S(2)}, u32[]{:S(2)}) %collective-permute-start.2) | collective-permute-done | bytes 34 | tf_op jit(solution)/shard_map/while/body/eval_jaxpr/ppermute | solution.py:18
  338.4 3.5 collective-permute-start.2
  342.0 7.5 %collective-permute-done.2 = bf16[1]{0:T(256)(128)(2,1)} collective-permute-done((bf16[1]{0:T(256)(128)(2,1)}, bf16[1]{0:T(256)(128)(2,1)}, u32[]{:S(2)}, u32[]{:S(2)}) %collective-permute-start.2) | collective-permute-done | bytes 34 | tf_op jit(solution)/shard_map/while/body/eval_jaxpr/ppermute | solution.py:18
  363.3 3.7 convolution_convert_fusion
  367.1 43.9 %reduce-scatter.2.cloned.1.call-done = bf16[128,2560]{1,0:T(8,128)(2,1)} async-done(((bf16[512,2560]{1,0:T(8,128)(2,1)}), bf16[128,2560]{1,0:T(8,128)(2,1)}) %reduce-scatter.2.cloned.1.call-update) | async-done | bytes 655376 | tf_op jit(solution)/shard_map/reduce_scatter | solution.py:130
  (342 shorter events, 149.8 us)
Async XLA Ops:
  6.5 44.0 %all-gather.3.cloned.1.call-start = ((), (), s32[]{:S(2)}) async-start(), calls=%async_computation.1 | async-start | bytes 3276800 | tf_op jit(solution)/shard_map/all_gather | solution.py:68
  10.2 400.9 %reduce-scatter.2.cloned.1.call-start = ((), (), s32[]{:S(2)}) async-start(), calls=%async_computation.2 | async-start | bytes 3276800 | tf_op jit(solution)/shard_map/reduce_scatter | solution.py:130
  83.7 15.6 %collective-permute-start = (bf16[512,1,128]{2,0,1:T(8,128)(2,1)}, bf16[512,1,128]{2,0,1:T(8,128)(2,1)S(1)}, u32[]{:S(2)}, u32[]{:S(2)}) collective-permute-start(bf16[512,1,128]{2,0,1:T(8,128)(2,1)} %get-tuple-element.259), channel_id=1, source_target_pairs={{252,0},{0,4},{4,8},{8,12},{12,16},{16,20},{20,24},{24,28},{28,32}... | collective-permute-start | bytes 393224 | tf_op jit(solution)/shard_map/while/body/eval_jaxpr/ppermute | solution.py:18
  84.9 18.3 %collective-permute-start.1 = (bf16[512,1,128]{2,0,1:T(8,128)(2,1)}, bf16[512,1,128]{2,0,1:T(8,128)(2,1)S(1)}, u32[]{:S(2)}, u32[]{:S(2)}) collective-permute-start(bf16[512,1,128]{2,0,1:T(8,128)(2,1)} %get-tuple-element.260), channel_id=1, source_target_pairs={{252,0},{0,4},{4,8},{8,12},{12,16},{16,20},{20,24},{24,28},{28,32}... | collective-permute-start | bytes 393224 | tf_op jit(solution)/shard_map/while/body/eval_jaxpr/ppermute | solution.py:18
  86.1 11.7 %collective-permute-start.2 = (bf16[1]{0:T(256)(128)(2,1)}, bf16[1]{0:T(256)(128)(2,1)}, u32[]{:S(2)}, u32[]{:S(2)}) collective-permute-start(bf16[1]{0:T(256)(128)(2,1)} %copy.49), channel_id=1, source_target_pairs={{252,0},{0,4},{4,8},{8,12},{12,16},{16,20},{20,24},{24,28},{28,32}... | collective-permute-start | bytes 14 | tf_op jit(solution)/shard_map/while/body/eval_jaxpr/ppermute | solution.py:18
  107.3 14.4 %collective-permute-start = (bf16[512,1,128]{2,0,1:T(8,128)(2,1)}, bf16[512,1,128]{2,0,1:T(8,128)(2,1)S(1)}, u32[]{:S(2)}, u32[]{:S(2)}) collective-permute-start(bf16[512,1,128]{2,0,1:T(8,128)(2,1)} %get-tuple-element.259), channel_id=1, source_target_pairs={{252,0},{0,4},{4,8},{8,12},{12,16},{16,20},{20,24},{24,28},{28,32}... | collective-permute-start | bytes 393224 | tf_op jit(solution)/shard_map/while/body/eval_jaxpr/ppermute | solution.py:18
  107.4 18.3 %collective-permute-start.1 = (bf16[512,1,128]{2,0,1:T(8,128)(2,1)}, bf16[512,1,128]{2,0,1:T(8,128)(2,1)S(1)}, u32[]{:S(2)}, u32[]{:S(2)}) collective-permute-start(bf16[512,1,128]{2,0,1:T(8,128)(2,1)} %get-tuple-element.260), channel_id=1, source_target_pairs={{252,0},{0,4},{4,8},{8,12},{12,16},{16,20},{20,24},{24,28},{28,32}... | collective-permute-start | bytes 393224 | tf_op jit(solution)/shard_map/while/body/eval_jaxpr/ppermute | solution.py:18
  107.5 12.8 %collective-permute-start.2 = (bf16[1]{0:T(256)(128)(2,1)}, bf16[1]{0:T(256)(128)(2,1)}, u32[]{:S(2)}, u32[]{:S(2)}) collective-permute-start(bf16[1]{0:T(256)(128)(2,1)} %copy.49), channel_id=1, source_target_pairs={{252,0},{0,4},{4,8},{8,12},{12,16},{16,20},{20,24},{24,28},{28,32}... | collective-permute-start | bytes 14 | tf_op jit(solution)/shard_map/while/body/eval_jaxpr/ppermute | solution.py:18
  129.8 13.3 %collective-permute-start = (bf16[512,1,128]{2,0,1:T(8,128)(2,1)}, bf16[512,1,128]{2,0,1:T(8,128)(2,1)S(1)}, u32[]{:S(2)}, u32[]{:S(2)}) collective-permute-start(bf16[512,1,128]{2,0,1:T(8,128)(2,1)} %get-tuple-element.259), channel_id=1, source_target_pairs={{252,0},{0,4},{4,8},{8,12},{12,16},{16,20},{20,24},{24,28},{28,32}... | collective-permute-start | bytes 393224 | tf_op jit(solution)/shard_map/while/body/eval_jaxpr/ppermute | solution.py:18
  129.9 17.2 %collective-permute-start.1 = (bf16[512,1,128]{2,0,1:T(8,128)(2,1)}, bf16[512,1,128]{2,0,1:T(8,128)(2,1)S(1)}, u32[]{:S(2)}, u32[]{:S(2)}) collective-permute-start(bf16[512,1,128]{2,0,1:T(8,128)(2,1)} %get-tuple-element.260), channel_id=1, source_target_pairs={{252,0},{0,4},{4,8},{8,12},{12,16},{16,20},{20,24},{24,28},{28,32}... | collective-permute-start | bytes 393224 | tf_op jit(solution)/shard_map/while/body/eval_jaxpr/ppermute | solution.py:18
  130.0 11.7 %collective-permute-start.2 = (bf16[1]{0:T(256)(128)(2,1)}, bf16[1]{0:T(256)(128)(2,1)}, u32[]{:S(2)}, u32[]{:S(2)}) collective-permute-start(bf16[1]{0:T(256)(128)(2,1)} %copy.49), channel_id=1, source_target_pairs={{252,0},{0,4},{4,8},{8,12},{12,16},{16,20},{20,24},{24,28},{28,32}... | collective-permute-start | bytes 14 | tf_op jit(solution)/shard_map/while/body/eval_jaxpr/ppermute | solution.py:18
  151.2 12.7 %collective-permute-start = (bf16[512,1,128]{2,0,1:T(8,128)(2,1)}, bf16[512,1,128]{2,0,1:T(8,128)(2,1)S(1)}, u32[]{:S(2)}, u32[]{:S(2)}) collective-permute-start(bf16[512,1,128]{2,0,1:T(8,128)(2,1)} %get-tuple-element.259), channel_id=1, source_target_pairs={{252,0},{0,4},{4,8},{8,12},{12,16},{16,20},{20,24},{24,28},{28,32}... | collective-permute-start | bytes 393224 | tf_op jit(solution)/shard_map/while/body/eval_jaxpr/ppermute | solution.py:18
  151.3 16.6 %collective-permute-start.1 = (bf16[512,1,128]{2,0,1:T(8,128)(2,1)}, bf16[512,1,128]{2,0,1:T(8,128)(2,1)S(1)}, u32[]{:S(2)}, u32[]{:S(2)}) collective-permute-start(bf16[512,1,128]{2,0,1:T(8,128)(2,1)} %get-tuple-element.260), channel_id=1, source_target_pairs={{252,0},{0,4},{4,8},{8,12},{12,16},{16,20},{20,24},{24,28},{28,32}... | collective-permute-start | bytes 393224 | tf_op jit(solution)/shard_map/while/body/eval_jaxpr/ppermute | solution.py:18
  172.0 12.7 %collective-permute-start = (bf16[512,1,128]{2,0,1:T(8,128)(2,1)}, bf16[512,1,128]{2,0,1:T(8,128)(2,1)S(1)}, u32[]{:S(2)}, u32[]{:S(2)}) collective-permute-start(bf16[512,1,128]{2,0,1:T(8,128)(2,1)} %get-tuple-element.259), channel_id=1, source_target_pairs={{252,0},{0,4},{4,8},{8,12},{12,16},{16,20},{20,24},{24,28},{28,32}... | collective-permute-start | bytes 393224 | tf_op jit(solution)/shard_map/while/body/eval_jaxpr/ppermute | solution.py:18
  172.1 16.6 %collective-permute-start.1 = (bf16[512,1,128]{2,0,1:T(8,128)(2,1)}, bf16[512,1,128]{2,0,1:T(8,128)(2,1)S(1)}, u32[]{:S(2)}, u32[]{:S(2)}) collective-permute-start(bf16[512,1,128]{2,0,1:T(8,128)(2,1)} %get-tuple-element.260), channel_id=1, source_target_pairs={{252,0},{0,4},{4,8},{8,12},{12,16},{16,20},{20,24},{24,28},{28,32}... | collective-permute-start | bytes 393224 | tf_op jit(solution)/shard_map/while/body/eval_jaxpr/ppermute | solution.py:18
  172.2 11.1 %collective-permute-start.2 = (bf16[1]{0:T(256)(128)(2,1)}, bf16[1]{0:T(256)(128)(2,1)}, u32[]{:S(2)}, u32[]{:S(2)}) collective-permute-start(bf16[1]{0:T(256)(128)(2,1)} %copy.49), channel_id=1, source_target_pairs={{252,0},{0,4},{4,8},{8,12},{12,16},{16,20},{20,24},{24,28},{28,32}... | collective-permute-start | bytes 14 | tf_op jit(solution)/shard_map/while/body/eval_jaxpr/ppermute | solution.py:18
  192.8 12.7 %collective-permute-start = (bf16[512,1,128]{2,0,1:T(8,128)(2,1)}, bf16[512,1,128]{2,0,1:T(8,128)(2,1)S(1)}, u32[]{:S(2)}, u32[]{:S(2)}) collective-permute-start(bf16[512,1,128]{2,0,1:T(8,128)(2,1)} %get-tuple-element.259), channel_id=1, source_target_pairs={{252,0},{0,4},{4,8},{8,12},{12,16},{16,20},{20,24},{24,28},{28,32}... | collective-permute-start | bytes 393224 | tf_op jit(solution)/shard_map/while/body/eval_jaxpr/ppermute | solution.py:18
  192.9 16.6 %collective-permute-start.1 = (bf16[512,1,128]{2,0,1:T(8,128)(2,1)}, bf16[512,1,128]{2,0,1:T(8,128)(2,1)S(1)}, u32[]{:S(2)}, u32[]{:S(2)}) collective-permute-start(bf16[512,1,128]{2,0,1:T(8,128)(2,1)} %get-tuple-element.260), channel_id=1, source_target_pairs={{252,0},{0,4},{4,8},{8,12},{12,16},{16,20},{20,24},{24,28},{28,32}... | collective-permute-start | bytes 393224 | tf_op jit(solution)/shard_map/while/body/eval_jaxpr/ppermute | solution.py:18
  213.6 12.7 %collective-permute-start = (bf16[512,1,128]{2,0,1:T(8,128)(2,1)}, bf16[512,1,128]{2,0,1:T(8,128)(2,1)S(1)}, u32[]{:S(2)}, u32[]{:S(2)}) collective-permute-start(bf16[512,1,128]{2,0,1:T(8,128)(2,1)} %get-tuple-element.259), channel_id=1, source_target_pairs={{252,0},{0,4},{4,8},{8,12},{12,16},{16,20},{20,24},{24,28},{28,32}... | collective-permute-start | bytes 393224 | tf_op jit(solution)/shard_map/while/body/eval_jaxpr/ppermute | solution.py:18
  213.6 16.6 %collective-permute-start.1 = (bf16[512,1,128]{2,0,1:T(8,128)(2,1)}, bf16[512,1,128]{2,0,1:T(8,128)(2,1)S(1)}, u32[]{:S(2)}, u32[]{:S(2)}) collective-permute-start(bf16[512,1,128]{2,0,1:T(8,128)(2,1)} %get-tuple-element.260), channel_id=1, source_target_pairs={{252,0},{0,4},{4,8},{8,12},{12,16},{16,20},{20,24},{24,28},{28,32}... | collective-permute-start | bytes 393224 | tf_op jit(solution)/shard_map/while/body/eval_jaxpr/ppermute | solution.py:18
  234.3 12.7 %collective-permute-start = (bf16[512,1,128]{2,0,1:T(8,128)(2,1)}, bf16[512,1,128]{2,0,1:T(8,128)(2,1)S(1)}, u32[]{:S(2)}, u32[]{:S(2)}) collective-permute-start(bf16[512,1,128]{2,0,1:T(8,128)(2,1)} %get-tuple-element.259), channel_id=1, source_target_pairs={{252,0},{0,4},{4,8},{8,12},{12,16},{16,20},{20,24},{24,28},{28,32}... | collective-permute-start | bytes 393224 | tf_op jit(solution)/shard_map/while/body/eval_jaxpr/ppermute | solution.py:18
  234.4 16.6 %collective-permute-start.1 = (bf16[512,1,128]{2,0,1:T(8,128)(2,1)}, bf16[512,1,128]{2,0,1:T(8,128)(2,1)S(1)}, u32[]{:S(2)}, u32[]{:S(2)}) collective-permute-start(bf16[512,1,128]{2,0,1:T(8,128)(2,1)} %get-tuple-element.260), channel_id=1, source_target_pairs={{252,0},{0,4},{4,8},{8,12},{12,16},{16,20},{20,24},{24,28},{28,32}... | collective-permute-start | bytes 393224 | tf_op jit(solution)/shard_map/while/body/eval_jaxpr/ppermute | solution.py:18
  255.1 12.7 %collective-permute-start = (bf16[512,1,128]{2,0,1:T(8,128)(2,1)}, bf16[512,1,128]{2,0,1:T(8,128)(2,1)S(1)}, u32[]{:S(2)}, u32[]{:S(2)}) collective-permute-start(bf16[512,1,128]{2,0,1:T(8,128)(2,1)} %get-tuple-element.259), channel_id=1, source_target_pairs={{252,0},{0,4},{4,8},{8,12},{12,16},{16,20},{20,24},{24,28},{28,32}... | collective-permute-start | bytes 393224 | tf_op jit(solution)/shard_map/while/body/eval_jaxpr/ppermute | solution.py:18
  255.2 16.6 %collective-permute-start.1 = (bf16[512,1,128]{2,0,1:T(8,128)(2,1)}, bf16[512,1,128]{2,0,1:T(8,128)(2,1)S(1)}, u32[]{:S(2)}, u32[]{:S(2)}) collective-permute-start(bf16[512,1,128]{2,0,1:T(8,128)(2,1)} %get-tuple-element.260), channel_id=1, source_target_pairs={{252,0},{0,4},{4,8},{8,12},{12,16},{16,20},{20,24},{24,28},{28,32}... | collective-permute-start | bytes 393224 | tf_op jit(solution)/shard_map/while/body/eval_jaxpr/ppermute | solution.py:18
  275.9 12.7 %collective-permute-start = (bf16[512,1,128]{2,0,1:T(8,128)(2,1)}, bf16[512,1,128]{2,0,1:T(8,128)(2,1)S(1)}, u32[]{:S(2)}, u32[]{:S(2)}) collective-permute-start(bf16[512,1,128]{2,0,1:T(8,128)(2,1)} %get-tuple-element.259), channel_id=1, source_target_pairs={{252,0},{0,4},{4,8},{8,12},{12,16},{16,20},{20,24},{24,28},{28,32}... | collective-permute-start | bytes 393224 | tf_op jit(solution)/shard_map/while/body/eval_jaxpr/ppermute | solution.py:18
  276.0 16.6 %collective-permute-start.1 = (bf16[512,1,128]{2,0,1:T(8,128)(2,1)}, bf16[512,1,128]{2,0,1:T(8,128)(2,1)S(1)}, u32[]{:S(2)}, u32[]{:S(2)}) collective-permute-start(bf16[512,1,128]{2,0,1:T(8,128)(2,1)} %get-tuple-element.260), channel_id=1, source_target_pairs={{252,0},{0,4},{4,8},{8,12},{12,16},{16,20},{20,24},{24,28},{28,32}... | collective-permute-start | bytes 393224 | tf_op jit(solution)/shard_map/while/body/eval_jaxpr/ppermute | solution.py:18
  296.7 12.7 %collective-permute-start = (bf16[512,1,128]{2,0,1:T(8,128)(2,1)}, bf16[512,1,128]{2,0,1:T(8,128)(2,1)S(1)}, u32[]{:S(2)}, u32[]{:S(2)}) collective-permute-start(bf16[512,1,128]{2,0,1:T(8,128)(2,1)} %get-tuple-element.259), channel_id=1, source_target_pairs={{252,0},{0,4},{4,8},{8,12},{12,16},{16,20},{20,24},{24,28},{28,32}... | collective-permute-start | bytes 393224 | tf_op jit(solution)/shard_map/while/body/eval_jaxpr/ppermute | solution.py:18
  296.8 16.6 %collective-permute-start.1 = (bf16[512,1,128]{2,0,1:T(8,128)(2,1)}, bf16[512,1,128]{2,0,1:T(8,128)(2,1)S(1)}, u32[]{:S(2)}, u32[]{:S(2)}) collective-permute-start(bf16[512,1,128]{2,0,1:T(8,128)(2,1)} %get-tuple-element.260), channel_id=1, source_target_pairs={{252,0},{0,4},{4,8},{8,12},{12,16},{16,20},{20,24},{24,28},{28,32}... | collective-permute-start | bytes 393224 | tf_op jit(solution)/shard_map/while/body/eval_jaxpr/ppermute | solution.py:18
  317.5 12.7 %collective-permute-start = (bf16[512,1,128]{2,0,1:T(8,128)(2,1)}, bf16[512,1,128]{2,0,1:T(8,128)(2,1)S(1)}, u32[]{:S(2)}, u32[]{:S(2)}) collective-permute-start(bf16[512,1,128]{2,0,1:T(8,128)(2,1)} %get-tuple-element.259), channel_id=1, source_target_pairs={{252,0},{0,4},{4,8},{8,12},{12,16},{16,20},{20,24},{24,28},{28,32}... | collective-permute-start | bytes 393224 | tf_op jit(solution)/shard_map/while/body/eval_jaxpr/ppermute | solution.py:18
  317.6 16.6 %collective-permute-start.1 = (bf16[512,1,128]{2,0,1:T(8,128)(2,1)}, bf16[512,1,128]{2,0,1:T(8,128)(2,1)S(1)}, u32[]{:S(2)}, u32[]{:S(2)}) collective-permute-start(bf16[512,1,128]{2,0,1:T(8,128)(2,1)} %get-tuple-element.260), channel_id=1, source_target_pairs={{252,0},{0,4},{4,8},{8,12},{12,16},{16,20},{20,24},{24,28},{28,32}... | collective-permute-start | bytes 393224 | tf_op jit(solution)/shard_map/while/body/eval_jaxpr/ppermute | solution.py:18
  338.3 12.7 %collective-permute-start = (bf16[512,1,128]{2,0,1:T(8,128)(2,1)}, bf16[512,1,128]{2,0,1:T(8,128)(2,1)S(1)}, u32[]{:S(2)}, u32[]{:S(2)}) collective-permute-start(bf16[512,1,128]{2,0,1:T(8,128)(2,1)} %get-tuple-element.259), channel_id=1, source_target_pairs={{252,0},{0,4},{4,8},{8,12},{12,16},{16,20},{20,24},{24,28},{28,32}... | collective-permute-start | bytes 393224 | tf_op jit(solution)/shard_map/while/body/eval_jaxpr/ppermute | solution.py:18
  338.3 16.6 %collective-permute-start.1 = (bf16[512,1,128]{2,0,1:T(8,128)(2,1)}, bf16[512,1,128]{2,0,1:T(8,128)(2,1)S(1)}, u32[]{:S(2)}, u32[]{:S(2)}) collective-permute-start(bf16[512,1,128]{2,0,1:T(8,128)(2,1)} %get-tuple-element.260), channel_id=1, source_target_pairs={{252,0},{0,4},{4,8},{8,12},{12,16},{16,20},{20,24},{24,28},{28,32}... | collective-permute-start | bytes 393224 | tf_op jit(solution)/shard_map/while/body/eval_jaxpr/ppermute | solution.py:18
  (74 other events, 660.9 us)
Sparse Core Ops, SparseCore 0:
  10.3 40.2 all-gather.2
  367.2 43.7 reduce-scatter.1
where the time goes:
time: 419 us; the launch traced here: 418 us
  waiting for transfers between devices  168 us (40%)
  matrix products  68 us (16%)
  starting transfers between devices  54 us (13%)
  local copies, waits for them, and re-layouts  47.3 us (11%)
  other arithmetic  39.7 us (9%)
  loops' own time  16.4 us (4%)
  between operations  16.1 us (4%)
  blocking collectives  8.07 us (2%)
    ppermute x39, waiting for transfers between devices, shifted(): return lax.ppermute(block, axis, route)  97.2 us
    ppermute x39, starting transfers between devices, shifted(): return lax.ppermute(block, axis, route)  54 us
    reduce_scatter x1, waiting for transfers between devices, local(): lax.psum_scatter(jnp.dot(mixed_heads, w_out, preferred_element_type=jnp.f...  43.9 us
    while x143, local copies, waits for them, and re-layouts  31.1 us
    dot_general x14, matrix products, attend(): jnp.einsum('qhgd,khd->hgqk', queries, key_blk, preferred_element_type=jnp...  29 us
    all_gather x1, waiting for transfers between devices, local(): piece = lax.all_gather(normed, 'inner', axis=0, tiled=True)  27.1 us
    dot_general x14, matrix products, attend(): jnp.einsum('hgqk,khd->hgqd', weights, value_blk, preferred_element_type=j...  25.6 us
    another operation x1, loops' own time, local(): lax.fori_loop(1, visit_count, advance, (key_heads, value_heads, own_run,...  16.4 us
  transfers between devices with their start and end apart: 41, of which 15 were waited for; matrix products, arithmetic and copies ran while one was open for 16% of the time, Pallas kernels for 0%

commit v1 on v0

v1 whole, which is shorter than its diff:
```python
import functools

import jax
import jax.numpy as jnp
from jax import lax
from jax.experimental import pallas as pl
from jax.experimental.pallas import tpu as pltpu
from jax.sharding import PartitionSpec as P

HEAD_DIM = 128
VISITS = 14
HALF = 256
SHARD = 128
STRIP = 128
HEADS = 5
TILE = 16
MSG = HALF + HALF + TILE
STATE = HEAD_DIM + 16
PEAK, TOTAL = HEAD_DIM, HEAD_DIM + 8

rope_base = 10000000.0
norm_eps = 1e-06
masked_score = -1e30
EXP_SCALE = HEAD_DIM ** (-0.5) * 1.4426950408889634
F32, BF16 = jnp.float32, jnp.bfloat16
VMEM_BYTES = 24 * 2**20

WHOLE = pl.BlockSpec(memory_space=pltpu.VMEM)
SCALARS = pl.BlockSpec(memory_space=pltpu.SMEM)


def params():
    return pltpu.CompilerParams(vmem_limit_bytes=VMEM_BYTES)


def cost(flops, data, exps=0):
    return pl.CostEstimate(flops=flops, bytes_accessed=data, transcendentals=exps)


def where_am_i(pos_ref, runs):
    first = pos_ref[0]
    run = lax.shift_right_logical(first, 8)
    second = run >= runs // 2
    lead = jnp.where(second, runs - 1 - run, run)
    core = lax.bitwise_and(lax.shift_right_logical(first, 7), 1)
    return lead, jnp.where(second, 1, 0), core


def norm_kernel(tokens_ref, gain_ref, out_ref):
    values = tokens_ref[...].astype(F32)
    scale = lax.rsqrt(jnp.mean(values * values, axis=-1, keepdims=True) + norm_eps)
    out_ref[...] = (values * scale * gain_ref[...][None, :]).astype(BF16)


def normalize(tokens, gain):
    return pl.pallas_call(
        norm_kernel,
        out_shape=jax.ShapeDtypeStruct(tokens.shape, BF16),
        in_specs=[WHOLE, WHOLE],
        out_specs=WHOLE,
        compiler_params=params(),
        cost_estimate=cost(5 * tokens.size, 4 * tokens.size),
    )(tokens, gain)


def gather_rows(pos_ref, runs, own_ref, other_ref, rows):
    lead, _, core = where_am_i(pos_ref, runs)
    rows[pl.ds(pl.multiple_of(core * SHARD, SHARD), SHARD), :] = own_ref[...]
    rows[pl.ds(pl.multiple_of((1 - core) * SHARD, SHARD), SHARD), :] = other_ref[...]
    return lead


def rope_for(half, cos_ref, sin_ref):
    lane = lax.broadcasted_iota(jnp.int32, (HALF, HEAD_DIM), 1)
    mine = (lane < HEAD_DIM // 2) if half == 0 else (lane >= HEAD_DIM // 2)
    cos, sin = cos_ref[...], sin_ref[...]
    cos = jnp.where(mine, cos, pltpu.roll(cos, HEAD_DIM // 2, 1))
    sin = jnp.where(mine, sin, pltpu.roll(sin, HEAD_DIM // 2, 1))
    sin = jnp.where(lane < HEAD_DIM // 2, -sin, sin)
    return lambda u: u * cos + pltpu.roll(u, HEAD_DIM // 2, 1) * sin


def key_kernel(half, runs, pos_ref, own_ref, other_ref, wk_ref, wv_ref, bk_ref, bv_ref, cos_ref, sin_ref,
               msg_ref, rows):
    lead = gather_rows(pos_ref, runs, own_ref, other_ref, rows)
    x = rows[...]
    rope = rope_for(half, cos_ref, sin_ref)
    keys = jnp.dot(x, wk_ref[...], preferred_element_type=F32) + bk_ref[...][None, :]
    msg_ref[0:HALF, :] = rope(keys).astype(BF16)
    values = jnp.dot(x, wv_ref[...], preferred_element_type=F32) + bv_ref[...][None, :]
    flipped = values.T.astype(BF16)
    msg_ref[HALF:HALF + SHARD, :] = flipped[:, 0:SHARD]
    msg_ref[HALF + SHARD:2 * HALF, :] = flipped[:, SHARD:HALF]
    msg_ref[2 * HALF:MSG, :] = jnp.full((TILE, HEAD_DIM), lead.astype(F32), F32).astype(BF16)


def query_kernel(half, runs, pos_ref, own_ref, other_ref, wq_ref, bq_ref, cos_ref, sin_ref, q_ref, rows):
    gather_rows(pos_ref, runs, own_ref, other_ref, rows)
    x = rows[...]
    rope = rope_for(half, cos_ref, sin_ref)
    for h in range(HEADS):
        cols = slice(h * HEAD_DIM, (h + 1) * HEAD_DIM)
        heads = jnp.dot(x, wq_ref[:, cols], preferred_element_type=F32) + bq_ref[cols][None, :]
        q_ref[:, h * HALF:(h + 1) * HALF] = rope(heads).T.astype(BF16)


def project_keys(half, runs, positions, own, other, weights, cos, sin):
    features = own.shape[1]
    return pl.pallas_call(
        functools.partial(key_kernel, half, runs),
        out_shape=jax.ShapeDtypeStruct((MSG, HEAD_DIM), BF16),
        in_specs=[SCALARS] + [WHOLE] * 8,
        out_specs=WHOLE,
        scratch_shapes=[pltpu.VMEM((HALF, features), BF16)],
        compiler_params=params(),
        cost_estimate=cost(4 * HALF * features * HEAD_DIM, 4 * features * HEAD_DIM),
    )(positions, own, other, *weights, cos, sin)


def project_queries(half, runs, positions, own, other, w_query, b_query, cos, sin):
    features = own.shape[1]
    return pl.pallas_call(
        functools.partial(query_kernel, half, runs),
        out_shape=jax.ShapeDtypeStruct((HEAD_DIM, HEADS * HALF), BF16),
        in_specs=[SCALARS] + [WHOLE] * 6,
        out_specs=WHOLE,
        scratch_shapes=[pltpu.VMEM((HALF, features), BF16)],
        compiler_params=params(),
        cost_estimate=cost(2 * HALF * features * HEADS * HEAD_DIM, 2 * features * HEADS * HEAD_DIM),
    )(positions, own, other, w_query, b_query, cos, sin)


def distance(kind, level, column):
    if kind == "up":
        return 4 * level + 0 * column
    if kind == "even":
        return 4 * level + column - lax.bitwise_xor(column, 1)
    if kind == "odd":
        return 4 * level + 2 * column - 3
    if kind == "cross":
        return 4 * level + jnp.where(column < 2, -2, 2)
    return jnp.where(column == 0, VISITS - 1, 0)


def visit(q, msgs, state, target, at, first=False):
    k = msgs[at, 0:HALF, :]
    vt = jnp.concatenate([msgs[at, HALF:HALF + SHARD, :], msgs[at, HALF + SHARD:2 * HALF, :]], axis=1)
    for strip in range(HEADS * HALF // STRIP):
        cols = slice(strip * STRIP, (strip + 1) * STRIP)
        s = jnp.dot(k, q[target, :, cols], preferred_element_type=F32)
        if first:
            key_at = lax.broadcasted_iota(jnp.int32, s.shape, 0)
            row_at = lax.broadcasted_iota(jnp.int32, s.shape, 1) + strip * STRIP % HALF
            s = jnp.where(key_at <= row_at, s, masked_score)
            peak = jnp.max(s, axis=0, keepdims=True)
        else:
            old = state[target, PEAK:PEAK + 1, cols]
            peak = jnp.maximum(old, jnp.max(s, axis=0, keepdims=True))
            factor = jnp.exp2((old - peak) * EXP_SCALE)
        expo = jnp.exp2((s - peak) * EXP_SCALE)
        total = jnp.sum(expo, axis=0, keepdims=True)
        mixed = jnp.dot(vt, expo.astype(BF16), preferred_element_type=F32)
        if not first:
            total = total + state[target, TOTAL:TOTAL + 1, cols] * factor
            mixed = mixed + state[target, 0:HEAD_DIM, cols] * factor
        state[target, PEAK:PEAK + 1, cols] = peak
        state[target, TOTAL:TOTAL + 1, cols] = total
        state[target, 0:HEAD_DIM, cols] = mixed


def attend_all(specs, pos_ref, runs, q, msgs, state, seen):
    lead, second, _ = where_am_i(pos_ref, runs)
    column = lax.bitwise_and(pos_ref[SHARD], 3)
    count = len(specs)
    for at, (_, kind, level) in enumerate(specs):
        back = distance(kind, level, column)
        valid = jnp.logical_and(back >= 1, back <= VISITS - 1)
        run = jnp.max(msgs[at, 2 * HALF:MSG, :].astype(F32)).astype(jnp.int32)
        seen[at] = jnp.where(valid, run, -1)

    def one(half, at):
        run = seen[at]
        role = second if half == 0 else 1 - second
        same = jnp.where(role == 0, run < lead, run > lead)

        @pl.when(jnp.logical_and(run >= 0, same))
        def _():
            visit(q, msgs, state, half, at)

        @pl.when(jnp.logical_and(run >= 0, role == 0))
        def _():
            visit(q, msgs, state, 1 - half, at)

    start = 0
    for half in (0, 1):
        stop = start + sum(1 for spec in specs if spec[0] == half)
        if stop > start:
            def body(at, carry, half=half):
                one(half, at)
                return carry
            lax.fori_loop(start, stop, body, 0)
        start = stop


def load(places, sources, qa_ref, qb_ref, q, msgs):
    q[0, :, :] = qa_ref[...]
    q[1, :, :] = qb_ref[...]
    for i, (which, at) in enumerate(places):
        msgs[i, :, :] = sources[which][at, :, :]


def attend_kernel(specs, places, own, runs, pos_ref, qa_ref, qb_ref, *rest):
    state, q, msgs, seen = rest[-4:]
    count = len(specs)
    if own:
        own_a, own_b, arrays = rest[0], rest[1], rest[2:-4]
        load(places, arrays, qa_ref, qb_ref, q, msgs)
        msgs[count, :, :] = own_a[0, :, :]
        msgs[count + 1, :, :] = own_b[0, :, :]
        _, second, _ = where_am_i(pos_ref, runs)
        for half in (0, 1):
            visit(q, msgs, state, half, count + half, True)
        visit(q, msgs, state, 1 - second, count + second)
    else:
        state_in, arrays = rest[0], rest[1:-4]
        load(places, arrays, qa_ref, qb_ref, q, msgs)
        state[...] = state_in[...]
    attend_all(specs, pos_ref, runs, q, msgs, state, seen)


def unpack(messages):
    arrays, places, specs = [], [], []
    for half, kind, level, array, at in sorted(messages, key=lambda m: m[0]):
        for i, known in enumerate(arrays):
            if known is array:
                break
        else:
            i = len(arrays)
            arrays.append(array)
        places.append((i, at))
        specs.append((half, kind, level))
    return tuple(specs), tuple(places), arrays


def working(count):
    return [
        pltpu.VMEM((2, HEAD_DIM, HEADS * HALF), BF16),
        pltpu.VMEM((count, MSG, HEAD_DIM), BF16),
        pltpu.SMEM((count,), jnp.int32),
    ]


def attend(messages, runs, positions, q, state=None, own=()):
    specs, places, arrays = unpack(messages)
    count = len(specs)
    before = list(own) if own else [state]
    return pl.pallas_call(
        functools.partial(attend_kernel, specs, places, bool(own), runs),
        out_shape=jax.ShapeDtypeStruct((2, STATE, HEADS * HALF), F32),
        in_specs=[SCALARS] + [WHOLE] * (2 + len(before) + len(arrays)),
        out_specs=WHOLE,
        scratch_shapes=working(count + len(own)),
        compiler_params=params(),
        cost_estimate=cost(count * 4 * HEADS * HALF * HALF * HEAD_DIM, 2**22, count * HEADS * HALF * HALF),
    )(positions, *q, *before, *arrays)


def project_out(pos_ref, half, mixed, w_ref, keep_ref, send_ref, runs):
    _, _, core = where_am_i(pos_ref, runs)
    keep_at = pl.ds(pl.multiple_of(core * SHARD, SHARD), SHARD)
    send_at = pl.ds(pl.multiple_of((1 - core) * SHARD, SHARD), SHARD)
    x = jnp.concatenate([mixed[send_at, :], mixed[keep_at, :]], axis=0)
    width = 512
    for j in range(w_ref.shape[1] // width):
        cols = slice(j * width, (j + 1) * width)
        part = jnp.dot(x, w_ref[:, cols], preferred_element_type=F32).astype(BF16)
        send_ref[:, cols] = part[0:SHARD]
        keep_ref[:, cols] = part[SHARD:HALF]


def last_kernel(specs, places, runs, pos_ref, qa_ref, qb_ref, state_in, w_ref, *rest):
    keep_far, send_far, near_ref, q, msgs, seen, state, mixed = rest[-8:]
    load(places, rest[:-8], qa_ref, qb_ref, q, msgs)
    state[...] = state_in[...]
    attend_all(specs, pos_ref, runs, q, msgs, state, seen)
    for half, to in ((1, mixed), (0, near_ref)):
        for h in range(HEADS):
            cols = slice(h * HALF, (h + 1) * HALF)
            scale = 1.0 / state[half, TOTAL:TOTAL + 1, cols]
            to[:, h * HEAD_DIM:(h + 1) * HEAD_DIM] = (state[half, 0:HEAD_DIM, cols] * scale).T.astype(BF16)
    project_out(pos_ref, 1, mixed, w_ref, keep_far, send_far, runs)


def attend_last(messages, runs, positions, q, state, w_out):
    specs, places, arrays = unpack(messages)
    count = len(specs)
    part = jax.ShapeDtypeStruct((SHARD, w_out.shape[1]), BF16)
    rows = (HALF, HEADS * HEAD_DIM)
    return pl.pallas_call(
        functools.partial(last_kernel, specs, places, runs),
        out_shape=(part, part, jax.ShapeDtypeStruct(rows, BF16)),
        in_specs=[SCALARS] + [WHOLE] * (4 + len(arrays)),
        out_specs=(WHOLE, WHOLE, WHOLE),
        scratch_shapes=working(count) + [pltpu.VMEM(state.shape, F32), pltpu.VMEM(rows, BF16)],
        compiler_params=params(),
        cost_estimate=cost(
            count * 4 * HEADS * HALF * HALF * HEAD_DIM + 2 * HALF * w_out.size, 2**23, count * HEADS * HALF * HALF
        ),
    )(positions, *q, state, w_out, *arrays)


def near_kernel(runs, pos_ref, mixed_ref, w_ref, keep_ref, send_ref):
    project_out(pos_ref, 0, mixed_ref, w_ref, keep_ref, send_ref, runs)


def near_out(runs, positions, mixed, w_out):
    part = jax.ShapeDtypeStruct((SHARD, w_out.shape[1]), BF16)
    return pl.pallas_call(
        functools.partial(near_kernel, runs),
        out_shape=(part, part),
        in_specs=[SCALARS, WHOLE, WHOLE],
        out_specs=(WHOLE, WHOLE),
        compiler_params=params(),
        cost_estimate=cost(2 * HALF * w_out.size, 2**22),
    )(positions, mixed, w_out)


def after(x, *earlier):
    return lax.optimization_barrier((x, *earlier))[0]


def local(tokens, norm_gain, w_query, b_query, w_key, b_key, w_value, b_value, w_out, positions):
    outer = lax.axis_size("outer")
    runs = 2 * outer

    def along(x, distance):
        return lax.ppermute(x, "outer", [(i, (i + distance) % outer) for i in range(outer)])

    def across(x, flip):
        return lax.ppermute(x, "inner", [(i, i ^ flip) for i in range(4)])

    normed = normalize(tokens, norm_gain)
    far = across(normed, 2)
    near = across(normed, 1)

    run = positions[0] // HALF
    positions = jnp.concatenate([positions, lax.axis_index("outer")[None]])
    row = jnp.arange(HALF, dtype=jnp.int32)[:, None]
    lane = jnp.arange(HEAD_DIM, dtype=jnp.int32)[None, :]
    places = jnp.where(lane < HEAD_DIM // 2, run, runs - 1 - run) * HALF + row
    inverse = rope_base ** (-(jnp.arange(HEAD_DIM // 2, dtype=F32) * 2.0 / HEAD_DIM))
    angles = places.astype(F32) * jnp.concatenate([inverse, inverse])[None, :]
    cos, sin = jnp.cos(angles), jnp.sin(angles)

    kv = (w_key, w_value, b_key, b_value)
    ring = range(outer)

    def pack(*parts):
        return jnp.concatenate(parts, axis=0)

    def up(x):
        return along(x, 4)

    def even(x):
        return lax.ppermute(x, "outer", [(i, i ^ 1) for i in ring])

    def odd(x):
        return lax.ppermute(x, "outer", [(i, i ^ 3) for i in ring])

    def cross(x):
        return lax.ppermute(x, "outer", [(i, i ^ 2) for i in ring if i % 4 >= 2])

    def corner(x):
        return lax.ppermute(x, "outer", [(i, (i + 1) % outer) for i in ring if i % 4 == 3])

    A, B = 0, 1

    a0 = project_keys(0, runs, positions, normed, near, kv, cos, sin)[None]
    a1, e0, o0 = up(a0), even(a0), odd(a0)
    qa = project_queries(0, runs, positions, after(normed, a0), near, w_query, b_query, cos, sin)

    far = after(far, qa, a1, e0, o0)
    far_near = across(far, 1)
    b0 = project_keys(1, runs, positions, far, far_near, kv, cos, sin)[None]
    u0 = pack(a1, b0)
    u1, e1, o1 = up(u0), even(pack(u0, o0)), odd(u0)
    qb = project_queries(1, runs, positions, after(far, b0), far_near, w_query, b_query, cos, sin)
    q = (qa, qb)
    state = attend(((A, "up", 1, a1, 0), (A, "even", 0, e0, 0), (A, "odd", 0, o0, 0)),
                   runs, positions, q, own=(a0, b0))

    v1 = after(u1, state)
    u2, e2, o2 = up(v1), even(pack(v1, o1[1:2])), odd(pack(v1, e1[0:1]))
    state = attend(((A, "up", 2, u1, 0), (B, "up", 1, u1, 1), (A, "even", 1, e1, 0), (B, "even", 0, e1, 1),
                    (A, "cross", 0, e1, 2), (A, "odd", 1, o1, 0), (B, "odd", 0, o1, 1)),
                   runs, positions, q, state)

    v2 = after(u2, state)
    u3, e3, o3 = up(v2[1:2]), even(pack(v2, o2[1:2])), odd(pack(v2, e2[0:1]))
    state = attend(((A, "up", 3, u2, 0), (B, "up", 2, u2, 1), (A, "even", 2, e2, 0), (B, "even", 1, e2, 1),
                    (B, "cross", 0, e2, 2), (A, "odd", 2, o2, 0), (B, "odd", 1, o2, 1), (A, "cross", 1, o2, 2)),
                   runs, positions, q, state)

    v3 = after(u3, state)
    e4, o4, c4, x4 = even(pack(v3, o3[1:2])), odd(pack(v3, e3[0:1])), corner(pack(v2[0:1], v3)), cross(v3)
    state = attend(((B, "up", 3, u3, 0), (A, "even", 3, e3, 0), (B, "even", 2, e3, 1), (B, "cross", 1, e3, 2),
                    (A, "odd", 3, o3, 0), (B, "odd", 2, o3, 1), (A, "cross", 2, o3, 2)),
                   runs, positions, q, state)
    messages = ((B, "even", 3, e4, 0), (B, "cross", 2, e4, 1), (B, "odd", 3, o4, 0), (A, "cross", 3, o4, 1),
                (A, "corner", 3, c4, 0), (B, "corner", 3, c4, 1), (B, "cross", 3, x4, 0))

    keep_far, send_far, mixed_near = attend_last(messages, runs, positions, q, state, w_out)
    got_far = across(send_far, 1)
    keep_near, send_near = near_out(runs, positions, mixed_near, w_out)
    got_near = across(send_near, 1)
    other = (keep_far.astype(F32) + got_far.astype(F32)).astype(BF16)
    arrived = across(other, 2)
    return (keep_near.astype(F32) + got_near.astype(F32) + arrived.astype(F32)).astype(BF16)


def solution(mesh):
    in_specs = (
        P(("outer", "inner"), None),
        P(),
        P(None, "inner"),
        P("inner"),
        P(None, "inner"),
        P("inner"),
        P(None, "inner"),
        P("inner"),
        P("inner", None),
        P(("outer", "inner")),
    )
    out_specs = P(("outer", "inner"), None)
    return jax.shard_map(local, mesh=mesh, in_specs=in_specs, out_specs=out_specs, check_vma=False)
```

time: 419 us -> 110 us (0.26)
  waiting for transfers between devices: 168 us -> 43.9 us
  matrix products: 68 us -> 0 us
  local copies, waits for them, and re-layouts: 47.3 us -> 2.01 us
  other arithmetic: 39.7 us -> 2.1 us
  Pallas kernels: 0 us -> 35.5 us
  starting transfers between devices: 54 us -> 25.3 us
  loops' own time: 16.4 us -> 0 us
  between operations: 16.1 us -> 0.47 us
  blocking collectives: 8.07 us -> 0 us
    dot_general x32 -> x0, matrix products: 68 us -> none  [the longest x14 29 us: attend(): jnp.einsum('qhgd,khd->hgqk', queries, key_blk, preferred_element_type=jnp...]
    ppermute x39 -> x22, waiting for transfers between devices: 97.2 us -> 43.9 us  [the longest x6 27.9 us: across(): return lax.ppermute(x, 'inner', [(i, i ^ flip) for i in range(4)])]
    reduce_scatter x1 -> x0, waiting for transfers between devices: 43.9 us -> none  [local(): lax.psum_scatter(jnp.dot(mixed_heads, w_out, preferred_element_type=jnp.f...]
    while x145 -> x0, local copies, waits for them, and re-layouts: 35.6 us -> none
    pallas_call x0 -> x11, Pallas kernels: none -> 35.5 us  [the longest x4 17.9 us: attend(): pl.pallas_call(functools.partial(attend_kernel, specs, places, bool(own),...]
    ppermute x39 -> x22, starting transfers between devices: 54 us -> 25.3 us  [the longest x6 11.4 us: across(): return lax.ppermute(x, 'inner', [(i, i ^ flip) for i in range(4)])]
    all_gather x1 -> x0, waiting for transfers between devices: 27.1 us -> none  [local(): piece = lax.all_gather(normed, 'inner', axis=0, tiled=True)]
    reduce_sum x15 -> x0, other arithmetic: 16.9 us -> none  [the longest x14 15.5 us: attend(): denominator = denominator * factor + jnp.sum(exponent, axis=-1)]
  transfers between devices with their start and end apart: 41 -> 22, of which waited for: 15 -> 10; matrix products, arithmetic and copies ran while one was open for 16% -> 1% of each run, Pallas kernels for 0% -> 24%
where the time goes in v1:
time: 110 us; the launch traced here: 109 us
  waiting for transfers between devices  43.9 us (40%)
  Pallas kernels  35.5 us (32%)
  starting transfers between devices  25.3 us (23%)
  other arithmetic  2.1 us (2%)
  local copies, waits for them, and re-layouts  2.01 us (2%)
    ppermute x6, waiting for transfers between devices, across(): return lax.ppermute(x, 'inner', [(i, i ^ flip) for i in range(4)])  27.9 us
    pallas_call x4, Pallas kernels, attend(): pl.pallas_call(functools.partial(attend_kernel, specs, places, bool(own),...  17.9 us
    ppermute x4, waiting for transfers between devices, along(): lax.ppermute(x, 'outer', [(i, (i + distance) % outer) for i in range(oute...  11.7 us
    ppermute x6, starting transfers between devices, across(): return lax.ppermute(x, 'inner', [(i, i ^ flip) for i in range(4)])  11.4 us
    ppermute x5, starting transfers between devices, odd(): return lax.ppermute(x, 'outer', [(i, i ^ 3) for i in ring])  7.67 us
    pallas_call x1, Pallas kernels, attend_last(): pl.pallas_call(functools.partial(last_kernel, specs, places, runs), out_s...  7.07 us
    pallas_call x2, Pallas kernels, project_queries(): pl.pallas_call(functools.partial(query_kernel, half, runs), out_shape=jax...  5.31 us
    ppermute x1, waiting for transfers between devices, corner(): lax.ppermute(x, 'outer', [(i, (i + 1) % outer) for i in ring if i % 4 == 3])  3.58 us
  transfers between devices with their start and end apart: 22, of which 10 were waited for; matrix products, arithmetic and copies ran while one was open for 1% of the time, Pallas kernels for 24%

profile of v1, /device:TPU:1, one launch (start us, length us, event | category | flops | bytes accessed | tf_op | source)
XLA Modules:
  0.0 109.3 jit_solution(10676908358115801025)
XLA Ops:
  0.0 1.2 %copy-done.4 = bf16[128,2560]{1,0:T(8,128)(2,1)S(1)} copy-done((bf16[128,2560]{1,0:T(8,128)(2,1)S(1)}, bf16[128,2560]{1,0:T(8,128)(2,1)}, u32[]{:S(2)}) %copy-start.4) | copy-done | bytes 655384
  2.3 3.3 %collective-permute-start = (bf16[128,2560]{1,0:T(8,128)(2,1)S(1)}, bf16[128,2560]{1,0:T(8,128)(2,1)S(1)}, u32[]{:S(2)}, u32[]{:S(2)}) collective-permute-start(bf16[128,2560]{1,0:T(8,128)(2,1)S(1)} %shard_map.100.own_ref), channel_id=1, source_target_pairs={{0,1},{1,0},{2,3},{3,2},{4,5},{5,4},{6,7},{7,6},{8,9},{9,8},{10,11... | collective-permute-start | bytes 1966088 | tf_op jit(solution)/shard_map/ppermute | solution.py:340
  7.3 1.5 %shard_map.101 = bf16[528,128]{1,0:T(8,128)(2,1)S(1)} custom-call(s32[129]{0:T(256)S(1)} %pad_add_fusion.pos_ref, bf16[128,2560]{1,0:T(8,128)(2,1)S(1)} %shard_map.100.own_ref, bf16[128,2560]{1,0:T(8,128)(2,1)S(1)} %collective-permute-done.other_ref, bf16[2560,128]{1,0:T(8,128)(2,1)S(1)} %copy-done.2, bf16[2560,128]{1,0:T(8,128)(2,1)S(1)} %copy-done.3, ...), custom_call_target="tpu_custom_call" | custom-call | flops 335544320 | bytes 1310720 | tf_op jit(solution)/shard_map/pallas_call | solution.py:109
  9.2 1.3 %collective-permute-start.3 = (bf16[1,528,128]{2,1,0:T(8,128)(2,1)S(1)}, bf16[1,528,128]{2,1,0:T(8,128)(2,1)S(1)}, u32[]{:S(2)}, u32[]{:S(2)}) collective-permute-start(bf16[1,528,128]{2,1,0:T(8,128)(2,1)S(1)} %bitcast.9), channel_id=1, source_target_pairs={{0,4},{4,0},{8,12},{12,8},{16,20},{20,16},{24,28},{28,24},{32,36},... | collective-permute-start | bytes 405512 | tf_op jit(solution)/shard_map/ppermute | solution.py:365
  10.5 1.9 %collective-permute-start.4 = (bf16[1,528,128]{2,1,0:T(8,128)(2,1)S(1)}, bf16[1,528,128]{2,1,0:T(8,128)(2,1)S(1)}, u32[]{:S(2)}, u32[]{:S(2)}) collective-permute-start(bf16[1,528,128]{2,1,0:T(8,128)(2,1)S(1)} %bitcast.10), channel_id=1, source_target_pairs={{0,12},{4,8},{8,4},{12,0},{16,28},{20,24},{24,20},{28,16},{32,44},... | collective-permute-start | bytes 405512 | tf_op jit(solution)/shard_map/ppermute | solution.py:368
  12.4 2.7 %shard_map.102.qa_ref = bf16[128,1280]{1,0:T(8,128)(2,1)S(1)} custom-call(s32[129]{0:T(256)S(1)} %pad_add_fusion.pos_ref, bf16[128,2560]{1,0:T(8,128)(2,1)S(1)} %shard_map.100.own_ref, bf16[128,2560]{1,0:T(8,128)(2,1)S(1)} %collective-permute-done.other_ref, bf16[2560,640]{1,0:T(8,128)(2,1)S(1)} %copy-done, f32[640]{0:T(1024)S(1)} %copy-done.5, ...), custom_call_target="tpu_custom_call" | custom-call | flops 838860800 | bytes 3276800 | tf_op jit(solution)/shard_map/pallas_call | solution.py:122
  15.0 9.7 %collective-permute-done.1.own_ref = bf16[128,2560]{1,0:T(8,128)(2,1)S(1)} collective-permute-done((bf16[128,2560]{1,0:T(8,128)(2,1)S(1)}, bf16[128,2560]{1,0:T(8,128)(2,1)S(1)}, u32[]{:S(2)}, u32[]{:S(2)}) %collective-permute-start.1) | collective-permute-done | bytes 655392 | tf_op jit(solution)/shard_map/ppermute | solution.py:340
  24.8 1.0 collective-permute-start.5
  25.7 1.7 %collective-permute-done.5.other_ref = bf16[128,2560]{1,0:T(8,128)(2,1)S(1)} collective-permute-done((bf16[128,2560]{1,0:T(8,128)(2,1)S(1)}, bf16[128,2560]{1,0:T(8,128)(2,1)S(1)}, u32[]{:S(2)}, u32[]{:S(2)}) %collective-permute-start.5) | collective-permute-done | bytes 655392 | tf_op jit(solution)/shard_map/ppermute | solution.py:340
  27.5 1.5 %shard_map.103 = bf16[528,128]{1,0:T(8,128)(2,1)S(1)} custom-call(s32[129]{0:T(256)S(1)} %pad_add_fusion.pos_ref, bf16[128,2560]{1,0:T(8,128)(2,1)S(1)} %collective-permute-done.1.own_ref, bf16[128,2560]{1,0:T(8,128)(2,1)S(1)} %collective-permute-done.5.other_ref, bf16[2560,128]{1,0:T(8,128)(2,1)S(1)} %copy-done.2, bf16[2560,128]{1,0:T(8,128)(2,1)S(1)} %copy-done.3, ...), custom_call_target="tpu_custom_call" | custom-call | flops 335544320 | bytes 1310720 | tf_op jit(solution)/shard_map/pallas_call | solution.py:109
  29.3 1.7 %collective-permute-start.8 = (bf16[2,528,128]{2,1,0:T(8,128)(2,1)S(1)}, bf16[2,528,128]{2,1,0:T(8,128)(2,1)S(1)}, u32[]{:S(2)}, u32[]{:S(2)}) collective-permute-start(bf16[2,528,128]{2,1,0:T(8,128)(2,1)S(1)} %pad_maximum_fusion.7), channel_id=1, source_target_pairs={{0,12},{4,8},{8,4},{12,0},{16,28},{20,24},{24,20},{28,16},{32,44},... | collective-permute-start | bytes 811016 | tf_op jit(solution)/shard_map/ppermute | solution.py:368
  31.0 2.7 %shard_map.104.qb_ref = bf16[128,1280]{1,0:T(8,128)(2,1)S(1)} custom-call(s32[129]{0:T(256)S(1)} %pad_add_fusion.pos_ref, bf16[128,2560]{1,0:T(8,128)(2,1)S(1)} %collective-permute-done.1.own_ref, bf16[128,2560]{1,0:T(8,128)(2,1)S(1)} %collective-permute-done.5.other_ref, bf16[2560,640]{1,0:T(8,128)(2,1)S(1)} %copy-done, f32[640]{0:T(1024)S(1)} %copy-done.5, ...), custom_call_target="tpu_custom_call" | custom-call | flops 838860800 | bytes 3276800 | tf_op jit(solution)/shard_map/pallas_call | solution.py:122
  33.7 3.4 %shard_map.105.rest_0_ = f32[2,144,1280]{2,1,0:T(8,128)S(1)} custom-call(s32[129]{0:T(256)S(1)} %pad_add_fusion.pos_ref, bf16[128,1280]{1,0:T(8,128)(2,1)S(1)} %shard_map.102.qa_ref, bf16[128,1280]{1,0:T(8,128)(2,1)S(1)} %shard_map.104.qb_ref, bf16[1,528,128]{2,1,0:T(8,128)(2,1)S(1)} %bitcast.11, bf16[1,528,128]{2,1,0:T(8,128)(2,1)S(1)} %bitcast.7, ...), custom_call_target="tpu_custom_call" | custom-call | flops 503316480 | bytes 4194304 | tf_op jit(solution)/shard_map/pallas_call | solution.py:257
  37.1 3.5 %collective-permute-done.6.rest_1_ = bf16[2,528,128]{2,1,0:T(8,128)(2,1)S(1)} collective-permute-done((bf16[2,528,128]{2,1,0:T(8,128)(2,1)S(1)}, bf16[2,528,128]{2,1,0:T(8,128)(2,1)S(1)}, u32[]{:S(2)}, u32[]{:S(2)}) %collective-permute-start.6) | collective-permute-done | bytes 270368 | tf_op jit(solution)/shard_map/ppermute | solution.py:337
  40.7 1.2 %collective-permute-start.10 = (bf16[3,528,128]{2,1,0:T(8,128)(2,1)S(1)}, bf16[3,528,128]{2,1,0:T(8,128)(2,1)S(1)}, u32[]{:S(2)}, u32[]{:S(2)}) collective-permute-start(bf16[3,528,128]{2,1,0:T(8,128)(2,1)S(1)} %get-tuple-element.32), channel_id=1, source_target_pairs={{0,4},{4,0},{8,12},{12,8},{16,20},{20,16},{24,28},{28,24},{32,36},... | collective-permute-start | bytes 1216520 | tf_op jit(solution)/shard_map/ppermute | solution.py:365
  41.9 1.1 %collective-permute-start.11 = (bf16[3,528,128]{2,1,0:T(8,128)(2,1)S(1)}, bf16[3,528,128]{2,1,0:T(8,128)(2,1)S(1)}, u32[]{:S(2)}, u32[]{:S(2)}) collective-permute-start(bf16[3,528,128]{2,1,0:T(8,128)(2,1)S(1)} %get-tuple-element.31), channel_id=1, source_target_pairs={{0,12},{4,8},{8,4},{12,0},{16,28},{20,24},{24,20},{28,16},{32,44},... | collective-permute-start | bytes 1216520 | tf_op jit(solution)/shard_map/ppermute | solution.py:368
  43.0 4.4 %shard_map.106.rest_0_ = f32[2,144,1280]{2,1,0:T(8,128)S(1)} custom-call(s32[129]{0:T(256)S(1)} %pad_add_fusion.pos_ref, bf16[128,1280]{1,0:T(8,128)(2,1)S(1)} %shard_map.102.qa_ref, bf16[128,1280]{1,0:T(8,128)(2,1)S(1)} %shard_map.104.qb_ref, f32[2,144,1280]{2,1,0:T(8,128)S(1)} %shard_map.105.rest_0_, ...), custom_call_target="tpu_custom_call" | custom-call | flops 1174405120 | bytes 4194304 | tf_op jit(solution)/shard_map/pallas_call | solution.py:257
  47.4 5.2 %collective-permute-done.9.rest_1_ = bf16[2,528,128]{2,1,0:T(8,128)(2,1)S(1)} collective-permute-done((bf16[2,528,128]{2,1,0:T(8,128)(2,1)S(1)}, bf16[2,528,128]{2,1,0:T(8,128)(2,1)S(1)}, u32[]{:S(2)}, u32[]{:S(2)}) %collective-permute-start.9) | collective-permute-done | bytes 270368 | tf_op jit(solution)/shard_map/ppermute | solution.py:337
  52.7 1.6 %collective-permute-start.13 = (bf16[3,528,128]{2,1,0:T(8,128)(2,1)S(1)}, bf16[3,528,128]{2,1,0:T(8,128)(2,1)S(1)}, u32[]{:S(2)}, u32[]{:S(2)}) collective-permute-start(bf16[3,528,128]{2,1,0:T(8,128)(2,1)S(1)} %get-tuple-element.29), channel_id=1, source_target_pairs={{0,12},{4,8},{8,4},{12,0},{16,28},{20,24},{24,20},{28,16},{32,44},... | collective-permute-start | bytes 1216520 | tf_op jit(solution)/shard_map/ppermute | solution.py:368
  54.6 4.4 %shard_map.107.rest_0_ = f32[2,144,1280]{2,1,0:T(8,128)S(1)} custom-call(s32[129]{0:T(256)S(1)} %pad_add_fusion.pos_ref, bf16[128,1280]{1,0:T(8,128)(2,1)S(1)} %shard_map.102.qa_ref, bf16[128,1280]{1,0:T(8,128)(2,1)S(1)} %shard_map.104.qb_ref, f32[2,144,1280]{2,1,0:T(8,128)S(1)} %shard_map.106.rest_0_, ...), custom_call_target="tpu_custom_call" | custom-call | flops 1342177280 | bytes 4194304 | tf_op jit(solution)/shard_map/pallas_call | solution.py:257
  59.0 3.1 %collective-permute-done.14.rest_3_ = bf16[1,528,128]{2,1,0:T(8,128)(2,1)S(1)} collective-permute-done((bf16[1,528,128]{2,1,0:T(8,128)(2,1)S(1)}, bf16[1,528,128]{2,1,0:T(8,128)(2,1)S(1)}, u32[]{:S(2)}, u32[]{:S(2)}) %collective-permute-start.14) | collective-permute-done | bytes 135200 | tf_op jit(solution)/shard_map/ppermute | solution.py:337
  62.2 1.4 %collective-permute-start.15 = (bf16[2,528,128]{2,1,0:T(8,128)(2,1)S(1)}, bf16[2,528,128]{2,1,0:T(8,128)(2,1)S(1)}, u32[]{:S(2)}, u32[]{:S(2)}) collective-permute-start(bf16[2,528,128]{2,1,0:T(8,128)(2,1)S(1)} %get-tuple-element.35), channel_id=1, source_target_pairs={{0,12},{4,8},{8,4},{12,0},{16,28},{20,24},{24,20},{28,16},{32,44},... | collective-permute-start | bytes 811016 | tf_op jit(solution)/shard_map/ppermute | solution.py:368
  63.5 1.3 %collective-permute-start.16 = (bf16[2,528,128]{2,1,0:T(8,128)(2,1)S(1)}, bf16[2,528,128]{2,1,0:T(8,128)(2,1)S(1)}, u32[]{:S(2)}, u32[]{:S(2)}) collective-permute-start(bf16[2,528,128]{2,1,0:T(8,128)(2,1)S(1)} %get-tuple-element.34), channel_id=1, source_target_pairs={{12,16},{28,32},{44,48},{60,64},{76,80},{92,96},{108,112},{124,128... | collective-permute-start | bytes 811016 | tf_op jit(solution)/shard_map/ppermute | solution.py:374
  65.1 1.4 %collective-permute-start.18 = (bf16[1,528,128]{2,1,0:T(8,128)(2,1)S(1)}, bf16[1,528,128]{2,1,0:T(8,128)(2,1)S(1)}, u32[]{:S(2)}, u32[]{:S(2)}) collective-permute-start(bf16[1,528,128]{2,1,0:T(8,128)(2,1)S(1)} %collective-permute-done.14.rest_3_), channel_id=1, source_target_pairs={{8,0},{12,4},{24,16},{28,20},{40,32},{44,36},{56,48},{60,52},{72,6... | collective-permute-start | bytes 405512 | tf_op jit(solution)/shard_map/ppermute | solution.py:371
  66.5 5.7 %shard_map.108.state_in = f32[2,144,1280]{2,1,0:T(8,128)S(1)} custom-call(s32[129]{0:T(256)S(1)} %pad_add_fusion.pos_ref, bf16[128,1280]{1,0:T(8,128)(2,1)S(1)} %shard_map.102.qa_ref, bf16[128,1280]{1,0:T(8,128)(2,1)S(1)} %shard_map.104.qb_ref, f32[2,144,1280]{2,1,0:T(8,128)S(1)} %shard_map.107.rest_0_, ...), custom_call_target="tpu_custom_call" | custom-call | flops 1174405120 | bytes 4194304 | tf_op jit(solution)/shard_map/pallas_call | solution.py:257
  72.9 3.6 %collective-permute-done.16.rest_1_ = bf16[2,528,128]{2,1,0:T(8,128)(2,1)S(1)} collective-permute-done((bf16[2,528,128]{2,1,0:T(8,128)(2,1)S(1)}, bf16[2,528,128]{2,1,0:T(8,128)(2,1)S(1)}, u32[]{:S(2)}, u32[]{:S(2)}) %collective-permute-start.16) | collective-permute-done | bytes 270368 | tf_op jit(solution)/shard_map/ppermute | solution.py:374
  76.5 7.1 %shard_map.109 = (bf16[128,2560]{1,0:T(8,128)(2,1)S(1)}, bf16[128,2560]{1,0:T(8,128)(2,1)S(1)}, bf16[256,640]{1,0:T(8,128)(2,1)S(1)}) custom-call(s32[129]{0:T(256)S(1)} %pad_add_fusion.pos_ref, bf16[128,1280]{1,0:T(8,128)(2,1)S(1)} %shard_map.102.qa_ref, bf16[128,1280]{1,0:T(8,128)(2,1)S(1)} %shard_map.104.qb_ref, f32[2,144,1280]{2,1,0:T(8,128)S(1)} %shard_map.108.state_in, ...), custom_call_target="tpu_custom_call" | custom-call | flops 2013265920 | bytes 8388608 | tf_op jit(solution)/shard_map/pallas_call | solution.py:299
  83.6 6.7 %collective-permute-start.20 = (bf16[128,2560]{1,0:T(8,128)(2,1)S(1)}, bf16[128,2560]{1,0:T(8,128)(2,1)S(1)}, u32[]{:S(2)}, u32[]{:S(2)}) collective-permute-start(bf16[128,2560]{1,0:T(8,128)(2,1)S(1)} %get-tuple-element.26), channel_id=1, source_target_pairs={{0,1},{1,0},{2,3},{3,2},{4,5},{5,4},{6,7},{7,6},{8,9},{9,8},{10,11... | collective-permute-start | bytes 1966088 | tf_op jit(solution)/shard_map/ppermute | solution.py:340
  90.3 1.7 %shard_map.110 = (bf16[128,2560]{1,0:T(8,128)(2,1)S(1)}, bf16[128,2560]{1,0:T(8,128)(2,1)S(1)}) custom-call(s32[129]{0:T(256)S(1)} %pad_add_fusion.pos_ref, bf16[256,640]{1,0:T(8,128)(2,1)S(1)} %get-tuple-element.22.mixed_ref, bf16[640,2560]{1,0:T(8,128)(2,1)S(1)} %copy-done.1), custom_call_target="tpu_custom_call" | custom-call | flops 838860800 | bytes 4194304 | tf_op jit(solution)/shard_map/pallas_call | solution.py:318
  92.7 1.5 %collective-permute-done.19 = bf16[128,2560]{1,0:T(8,128)(2,1)S(1)} collective-permute-done((bf16[128,2560]{1,0:T(8,128)(2,1)S(1)}, bf16[128,2560]{1,0:T(8,128)(2,1)S(1)}, u32[]{:S(2)}, u32[]{:S(2)}) %collective-permute-start.19) | collective-permute-done | bytes 655392 | tf_op jit(solution)/shard_map/ppermute | solution.py:340
  94.2 14.0 %collective-permute-done.21 = bf16[128,2560]{1,0:T(8,128)(2,1)S(1)} collective-permute-done((bf16[128,2560]{1,0:T(8,128)(2,1)S(1)}, bf16[128,2560]{1,0:T(8,128)(2,1)S(1)}, u32[]{:S(2)}, u32[]{:S(2)}) %collective-permute-start.21) | collective-permute-done | bytes 655392 | tf_op jit(solution)/shard_map/ppermute | solution.py:340
  108.2 1.1 %add_convert_fusion = bf16[128,2560]{1,0:T(8,128)(2,1)} fusion(bf16[128,2560]{1,0:T(8,128)(2,1)S(1)} %collective-permute-done.21, bf16[128,2560]{1,0:T(8,128)(2,1)S(1)} %collective-permute-done.19, bf16[128,2560]{1,0:T(8,128)(2,1)S(1)} %get-tuple-element.23), kind=kLoop, calls=%fused_computation | loop fusion | flops 1966080 | bytes 2621440 | tf_op jit(solution)/shard_map/convert_element_type | solution.py:418
  (62 shorter events, 5.3 us)
Async XLA Ops:
  0.0 7.3 %copy-start.2 = (bf16[2560,128]{1,0:T(8,128)(2,1)S(1)}, bf16[2560,128]{1,0:T(8,128)(2,1)}, u32[]{:S(2)}) copy-start(bf16[2560,128]{1,0:T(8,128)(2,1)} %wk_ref.3) | copy-start | bytes 1966084
  0.0 7.3 %copy-start.3 = (bf16[2560,128]{1,0:T(8,128)(2,1)S(1)}, bf16[2560,128]{1,0:T(8,128)(2,1)}, u32[]{:S(2)}) copy-start(bf16[2560,128]{1,0:T(8,128)(2,1)} %wv_ref.3) | copy-start | bytes 1966084
  0.0 1.2 %copy-start.4 = (bf16[128,2560]{1,0:T(8,128)(2,1)S(1)}, bf16[128,2560]{1,0:T(8,128)(2,1)}, u32[]{:S(2)}) copy-start(bf16[128,2560]{1,0:T(8,128)(2,1)} %tokens_ref.1) | copy-start | bytes 1966084
  1.2 0.7 copy-start.6
  1.9 3.8 %copy-start.9 = (s32[128]{0:T(128)S(1)}, s32[128]{0:T(128)}, u32[]{:S(2)}) copy-start(s32[128]{0:T(128)} %param.19) | copy-start | bytes 1540
  1.9 5.4 %copy-start.7 = (f32[128]{0:T(128)S(1)}, f32[128]{0:T(128)}, u32[]{:S(2)}) copy-start(f32[128]{0:T(128)} %bk_ref.3) | copy-start | bytes 1540
  1.9 5.4 %copy-start.8 = (f32[128]{0:T(128)S(1)}, f32[128]{0:T(128)}, u32[]{:S(2)}) copy-start(f32[128]{0:T(128)} %bv_ref.3) | copy-start | bytes 1540
  2.3 5.1 %collective-permute-start = (bf16[128,2560]{1,0:T(8,128)(2,1)S(1)}, bf16[128,2560]{1,0:T(8,128)(2,1)S(1)}, u32[]{:S(2)}, u32[]{:S(2)}) collective-permute-start(bf16[128,2560]{1,0:T(8,128)(2,1)S(1)} %shard_map.100.own_ref), channel_id=1, source_target_pairs={{0,1},{1,0},{2,3},{3,2},{4,5},{5,4},{6,7},{7,6},{8,9},{9,8},{10,11... | collective-permute-start | bytes 1966088 | tf_op jit(solution)/shard_map/ppermute | solution.py:340
  5.6 19.2 %collective-permute-start.1 = (bf16[128,2560]{1,0:T(8,128)(2,1)S(1)}, bf16[128,2560]{1,0:T(8,128)(2,1)S(1)}, u32[]{:S(2)}, u32[]{:S(2)}) collective-permute-start(bf16[128,2560]{1,0:T(8,128)(2,1)S(1)} %shard_map.100.own_ref), channel_id=1, source_target_pairs={{0,2},{1,3},{2,0},{3,1},{4,6},{5,7},{6,4},{7,5},{8,10},{9,11},{10,... | collective-permute-start | bytes 1966088 | tf_op jit(solution)/shard_map/ppermute | solution.py:340
  5.9 6.5 %copy-start = (bf16[2560,640]{1,0:T(8,128)(2,1)S(1)}, bf16[2560,640]{1,0:T(8,128)(2,1)}, u32[]{:S(2)}) copy-start(bf16[2560,640]{1,0:T(8,128)(2,1)} %wq_ref.3) | copy-start | bytes 9830404
  7.3 5.1 %copy-start.5 = (f32[640]{0:T(1024)S(1)}, f32[640]{0:T(1024)}, u32[]{:S(2)}) copy-start(f32[640]{0:T(1024)} %bq_ref.3) | copy-start | bytes 7684
  8.9 15.9 %collective-permute-start.2 = (bf16[1,528,128]{2,1,0:T(8,128)(2,1)S(1)}, bf16[1,528,128]{2,1,0:T(8,128)(2,1)S(1)}, u32[]{:S(2)}, u32[]{:S(2)}) collective-permute-start(bf16[1,528,128]{2,1,0:T(8,128)(2,1)S(1)} %bitcast.8), channel_id=1, source_target_pairs={{0,16},{4,20},{8,24},{12,28},{16,32},{20,36},{24,40},{28,44},{32,4... | collective-permute-start | bytes 405512 | tf_op jit(solution)/shard_map/ppermute | solution.py:337
  9.2 15.6 %collective-permute-start.3 = (bf16[1,528,128]{2,1,0:T(8,128)(2,1)S(1)}, bf16[1,528,128]{2,1,0:T(8,128)(2,1)S(1)}, u32[]{:S(2)}, u32[]{:S(2)}) collective-permute-start(bf16[1,528,128]{2,1,0:T(8,128)(2,1)S(1)} %bitcast.9), channel_id=1, source_target_pairs={{0,4},{4,0},{8,12},{12,8},{16,20},{20,16},{24,28},{28,24},{32,36},... | collective-permute-start | bytes 405512 | tf_op jit(solution)/shard_map/ppermute | solution.py:365
  10.5 14.3 %collective-permute-start.4 = (bf16[1,528,128]{2,1,0:T(8,128)(2,1)S(1)}, bf16[1,528,128]{2,1,0:T(8,128)(2,1)S(1)}, u32[]{:S(2)}, u32[]{:S(2)}) collective-permute-start(bf16[1,528,128]{2,1,0:T(8,128)(2,1)S(1)} %bitcast.10), channel_id=1, source_target_pairs={{0,12},{4,8},{8,4},{12,0},{16,28},{20,24},{24,20},{28,16},{32,44},... | collective-permute-start | bytes 405512 | tf_op jit(solution)/shard_map/ppermute | solution.py:368
  24.8 2.7 %collective-permute-start.5 = (bf16[128,2560]{1,0:T(8,128)(2,1)S(1)}, bf16[128,2560]{1,0:T(8,128)(2,1)S(1)}, u32[]{:S(2)}, u32[]{:S(2)}) collective-permute-start(bf16[128,2560]{1,0:T(8,128)(2,1)S(1)} %collective-permute-done.1.own_ref), channel_id=1, source_target_pairs={{0,1},{1,0},{2,3},{3,2},{4,5},{5,4},{6,7},{7,6},{8,9},{9,8},{10,11... | collective-permute-start | bytes 1966088 | tf_op jit(solution)/shard_map/ppermute | solution.py:340
  29.1 11.5 %collective-permute-start.7 = (bf16[3,528,128]{2,1,0:T(8,128)(2,1)S(1)}, bf16[3,528,128]{2,1,0:T(8,128)(2,1)S(1)}, u32[]{:S(2)}, u32[]{:S(2)}) collective-permute-start(bf16[3,528,128]{2,1,0:T(8,128)(2,1)S(1)} %pad_maximum_fusion.4), channel_id=1, source_target_pairs={{0,4},{4,0},{8,12},{12,8},{16,20},{20,16},{24,28},{28,24},{32,36},... | collective-permute-start | bytes 1216520 | tf_op jit(solution)/shard_map/ppermute | solution.py:365
  29.2 11.4 %collective-permute-start.6 = (bf16[2,528,128]{2,1,0:T(8,128)(2,1)S(1)}, bf16[2,528,128]{2,1,0:T(8,128)(2,1)S(1)}, u32[]{:S(2)}, u32[]{:S(2)}) collective-permute-start(bf16[2,528,128]{2,1,0:T(8,128)(2,1)S(1)} %pad_maximum_fusion.7), channel_id=1, source_target_pairs={{0,16},{4,20},{8,24},{12,28},{16,32},{20,36},{24,40},{28,44},{32,4... | collective-permute-start | bytes 811016 | tf_op jit(solution)/shard_map/ppermute | solution.py:337
  29.3 11.3 %collective-permute-start.8 = (bf16[2,528,128]{2,1,0:T(8,128)(2,1)S(1)}, bf16[2,528,128]{2,1,0:T(8,128)(2,1)S(1)}, u32[]{:S(2)}, u32[]{:S(2)}) collective-permute-start(bf16[2,528,128]{2,1,0:T(8,128)(2,1)S(1)} %pad_maximum_fusion.7), channel_id=1, source_target_pairs={{0,12},{4,8},{8,4},{12,0},{16,28},{20,24},{24,20},{28,16},{32,44},... | collective-permute-start | bytes 811016 | tf_op jit(solution)/shard_map/ppermute | solution.py:368
  40.7 11.9 %collective-permute-start.10 = (bf16[3,528,128]{2,1,0:T(8,128)(2,1)S(1)}, bf16[3,528,128]{2,1,0:T(8,128)(2,1)S(1)}, u32[]{:S(2)}, u32[]{:S(2)}) collective-permute-start(bf16[3,528,128]{2,1,0:T(8,128)(2,1)S(1)} %get-tuple-element.32), channel_id=1, source_target_pairs={{0,4},{4,0},{8,12},{12,8},{16,20},{20,16},{24,28},{28,24},{32,36},... | collective-permute-start | bytes 1216520 | tf_op jit(solution)/shard_map/ppermute | solution.py:365
  41.9 10.7 %collective-permute-start.11 = (bf16[3,528,128]{2,1,0:T(8,128)(2,1)S(1)}, bf16[3,528,128]{2,1,0:T(8,128)(2,1)S(1)}, u32[]{:S(2)}, u32[]{:S(2)}) collective-permute-start(bf16[3,528,128]{2,1,0:T(8,128)(2,1)S(1)} %get-tuple-element.31), channel_id=1, source_target_pairs={{0,12},{4,8},{8,4},{12,0},{16,28},{20,24},{24,20},{28,16},{32,44},... | collective-permute-start | bytes 1216520 | tf_op jit(solution)/shard_map/ppermute | solution.py:368
  43.0 9.6 %collective-permute-start.9 = (bf16[2,528,128]{2,1,0:T(8,128)(2,1)S(1)}, bf16[2,528,128]{2,1,0:T(8,128)(2,1)S(1)}, u32[]{:S(2)}, u32[]{:S(2)}) collective-permute-start(bf16[2,528,128]{2,1,0:T(8,128)(2,1)S(1)} %collective-permute-done.6.rest_1_), channel_id=1, source_target_pairs={{0,16},{4,20},{8,24},{12,28},{16,32},{20,36},{24,40},{28,44},{32,4... | collective-permute-start | bytes 811016 | tf_op jit(solution)/shard_map/ppermute | solution.py:337
  52.7 9.4 %collective-permute-start.13 = (bf16[3,528,128]{2,1,0:T(8,128)(2,1)S(1)}, bf16[3,528,128]{2,1,0:T(8,128)(2,1)S(1)}, u32[]{:S(2)}, u32[]{:S(2)}) collective-permute-start(bf16[3,528,128]{2,1,0:T(8,128)(2,1)S(1)} %get-tuple-element.29), channel_id=1, source_target_pairs={{0,12},{4,8},{8,4},{12,0},{16,28},{20,24},{24,20},{28,16},{32,44},... | collective-permute-start | bytes 1216520 | tf_op jit(solution)/shard_map/ppermute | solution.py:368
  54.3 7.8 %collective-permute-start.12 = (bf16[3,528,128]{2,1,0:T(8,128)(2,1)S(1)}, bf16[3,528,128]{2,1,0:T(8,128)(2,1)S(1)}, u32[]{:S(2)}, u32[]{:S(2)}) collective-permute-start(bf16[3,528,128]{2,1,0:T(8,128)(2,1)S(1)} %get-tuple-element.30), channel_id=1, source_target_pairs={{0,4},{4,0},{8,12},{12,8},{16,20},{20,16},{24,28},{28,24},{32,36},... | collective-permute-start | bytes 1216520 | tf_op jit(solution)/shard_map/ppermute | solution.py:365
  54.3 7.8 %collective-permute-start.14 = (bf16[1,528,128]{2,1,0:T(8,128)(2,1)S(1)}, bf16[1,528,128]{2,1,0:T(8,128)(2,1)S(1)}, u32[]{:S(2)}, u32[]{:S(2)}) collective-permute-start(bf16[1,528,128]{2,1,0:T(8,128)(2,1)S(1)} %get-tuple-element.28), channel_id=1, source_target_pairs={{0,16},{4,20},{8,24},{12,28},{16,32},{20,36},{24,40},{28,44},{32,4... | collective-permute-start | bytes 405512 | tf_op jit(solution)/shard_map/ppermute | solution.py:337
  62.2 10.7 %collective-permute-start.15 = (bf16[2,528,128]{2,1,0:T(8,128)(2,1)S(1)}, bf16[2,528,128]{2,1,0:T(8,128)(2,1)S(1)}, u32[]{:S(2)}, u32[]{:S(2)}) collective-permute-start(bf16[2,528,128]{2,1,0:T(8,128)(2,1)S(1)} %get-tuple-element.35), channel_id=1, source_target_pairs={{0,12},{4,8},{8,4},{12,0},{16,28},{20,24},{24,20},{28,16},{32,44},... | collective-permute-start | bytes 811016 | tf_op jit(solution)/shard_map/ppermute | solution.py:368
  63.5 13.0 %collective-permute-start.16 = (bf16[2,528,128]{2,1,0:T(8,128)(2,1)S(1)}, bf16[2,528,128]{2,1,0:T(8,128)(2,1)S(1)}, u32[]{:S(2)}, u32[]{:S(2)}) collective-permute-start(bf16[2,528,128]{2,1,0:T(8,128)(2,1)S(1)} %get-tuple-element.34), channel_id=1, source_target_pairs={{12,16},{28,32},{44,48},{60,64},{76,80},{92,96},{108,112},{124,128... | collective-permute-start | bytes 811016 | tf_op jit(solution)/shard_map/ppermute | solution.py:374
  64.8 11.7 %copy-start.1 = (bf16[640,2560]{1,0:T(8,128)(2,1)S(1)}, bf16[640,2560]{1,0:T(8,128)(2,1)}, u32[]{:S(2)}) copy-start(bf16[640,2560]{1,0:T(8,128)(2,1)} %w_ref.3) | copy-start | bytes 9830404
  64.8 11.7 %collective-permute-start.17 = (bf16[2,528,128]{2,1,0:T(8,128)(2,1)S(1)}, bf16[2,528,128]{2,1,0:T(8,128)(2,1)S(1)}, u32[]{:S(2)}, u32[]{:S(2)}) collective-permute-start(bf16[2,528,128]{2,1,0:T(8,128)(2,1)S(1)} %get-tuple-element.33), channel_id=1, source_target_pairs={{0,4},{4,0},{8,12},{12,8},{16,20},{20,16},{24,28},{28,24},{32,36},... | collective-permute-start | bytes 811016 | tf_op jit(solution)/shard_map/ppermute | solution.py:365
  65.1 7.8 %collective-permute-start.18 = (bf16[1,528,128]{2,1,0:T(8,128)(2,1)S(1)}, bf16[1,528,128]{2,1,0:T(8,128)(2,1)S(1)}, u32[]{:S(2)}, u32[]{:S(2)}) collective-permute-start(bf16[1,528,128]{2,1,0:T(8,128)(2,1)S(1)} %collective-permute-done.14.rest_3_), channel_id=1, source_target_pairs={{8,0},{12,4},{24,16},{28,20},{40,32},{44,36},{56,48},{60,52},{72,6... | collective-permute-start | bytes 405512 | tf_op jit(solution)/shard_map/ppermute | solution.py:371
  83.6 8.5 %collective-permute-start.20 = (bf16[128,2560]{1,0:T(8,128)(2,1)S(1)}, bf16[128,2560]{1,0:T(8,128)(2,1)S(1)}, u32[]{:S(2)}, u32[]{:S(2)}) collective-permute-start(bf16[128,2560]{1,0:T(8,128)(2,1)S(1)} %get-tuple-element.26), channel_id=1, source_target_pairs={{0,1},{1,0},{2,3},{3,2},{4,5},{5,4},{6,7},{7,6},{8,9},{9,8},{10,11... | collective-permute-start | bytes 1966088 | tf_op jit(solution)/shard_map/ppermute | solution.py:340
  92.0 2.2 %collective-permute-start.19 = (bf16[128,2560]{1,0:T(8,128)(2,1)S(1)}, bf16[128,2560]{1,0:T(8,128)(2,1)S(1)}, u32[]{:S(2)}, u32[]{:S(2)}) collective-permute-start(bf16[128,2560]{1,0:T(8,128)(2,1)S(1)} %get-tuple-element.24), channel_id=1, source_target_pairs={{0,1},{1,0},{2,3},{3,2},{4,5},{5,4},{6,7},{7,6},{8,9},{9,8},{10,11... | collective-permute-start | bytes 1966088 | tf_op jit(solution)/shard_map/ppermute | solution.py:340
  92.3 15.9 %collective-permute-start.21 = (bf16[128,2560]{1,0:T(8,128)(2,1)S(1)}, bf16[128,2560]{1,0:T(8,128)(2,1)S(1)}, u32[]{:S(2)}, u32[]{:S(2)}) collective-permute-start(bf16[128,2560]{1,0:T(8,128)(2,1)S(1)} %add_convert_fusion.1), channel_id=1, source_target_pairs={{0,2},{1,3},{2,0},{3,1},{4,6},{5,7},{6,4},{7,5},{8,10},{9,11},{10,... | collective-permute-start | bytes 1966088 | tf_op jit(solution)/shard_map/ppermute | solution.py:340
